TPU v7x, 32 devices: a whole 2x2x4 slice. The times are simulated.
32 devices in a mesh: wide: 8 (over z, y), narrow: 4 (over x, core).
Axes of the slice: x: 2, y: 2, z: 4, core: 2. Of those that a mesh axis runs over, the one named last changes fastest.
Arguments:
- points: bfloat16 [256, 256, 256], P('wide', 'narrow'), may hold values from -6 to 6
- targets: bfloat16 [256, 256, 256], P('wide', 'narrow'), may hold values from -6 to 6
- centroids: float32 [128, 256], P('wide'), may hold values from -3 to 3
- block_list: int32 [256], P('wide'), may hold values from 0 to 15
- lengths: int32 [256], P('wide'), may hold values from 1 to 256
- sources: int32 [256], P('wide'), may hold values from 0 to 255, as said below
Outputs:
- rotated: bfloat16 [256, 256, 256], P('wide', 'narrow')
Inputs may be any that keep to these rules, and one draw needn't show every extreme that they name: For every index w of wide and slot j below 2, sources[w * 32 + j] = u * 32 + j for some index u of wide, each such input block named exactly once; every other entry names its own position.
All inputs are finite; a program needn't handle non-finite values.
Results may differ from a plain program's by a relative error of at most 0.0051.
Values may be sent and summed in bfloat16 or wider, within the bound.
No kernel may reach another device: no remote copies, remote signals or barrier semaphores. Data moves between devices by JAX's collectives and lax.ppermute only.
A program may use at most 64 MiB of HBM per device.

v0:
```python
import jax
import jax.numpy as jnp
from jax import lax
from jax.sharding import PartitionSpec as P

MOVE = 2
ITERS = 5


highest_prec = lax.Precision.HIGHEST


def newton_polar(cross_gram):
    frob_norm = jnp.sqrt(jnp.sum(cross_gram * cross_gram, axis=(1, 2), keepdims=True) + 1e-06)
    polar_iter = cross_gram / frob_norm
    for sweep_index in range(ITERS):
        product = jnp.einsum("lde,lfe->ldf", polar_iter, polar_iter, precision=highest_prec)
        polar_iter = 1.5 * polar_iter - 0.5 * jnp.einsum(
            "ldf,lfe->lde", product, polar_iter, precision=highest_prec
        )
    return polar_iter.astype(jnp.bfloat16)


def local(points, targets, centroids, block_list, lengths, sources):
    block_count, rows_here, embed_width = points.shape
    list_count = centroids.shape[0]
    row_index = lax.axis_index("narrow") * rows_here + jnp.arange(rows_here, dtype=jnp.int32)
    in_range = row_index[None, :] < lengths[:, None]
    list_match = block_list[:, None] == jnp.arange(list_count, dtype=jnp.int32)[None, :]
    list_pick = list_match.astype(jnp.float32)
    centre_rows = jnp.dot(list_pick, centroids, precision=highest_prec)
    residual = jnp.where(
        in_range[:, :, None], points.astype(jnp.float32) - centre_rows[:, None, :], 0.0
    ).astype(jnp.bfloat16)
    block_grams = jnp.einsum("brd,bre->bde", residual, targets, preferred_element_type=jnp.float32)
    cross_gram = lax.psum_scatter(
        jnp.einsum("bl,bde->lde", list_pick, block_grams, precision=highest_prec),
        "narrow",
        scatter_dimension=0,
        tiled=True,
    )
    rotation = newton_polar(cross_gram)
    all_rotations = lax.all_gather(rotation, "narrow", axis=0, tiled=True)
    chosen = jnp.einsum(
        "bl,lde->bde",
        list_match.astype(jnp.bfloat16),
        all_rotations,
        preferred_element_type=jnp.float32,
    ).astype(jnp.bfloat16)
    turned = jnp.einsum(
        "brd,bde->bre", residual, chosen, preferred_element_type=jnp.float32
    ).astype(jnp.bfloat16)
    donor_index = sources[:MOVE] // block_count
    part_rows = lax.all_gather(turned[None, :MOVE], "wide", axis=0, tiled=True)
    how_many = part_rows.shape[0]
    selector = (donor_index[:, None] == jnp.arange(how_many, dtype=jnp.int32)[None, :]).astype(
        jnp.bfloat16
    )
    handed = jnp.einsum("ji,ijrd->jrd", selector, part_rows, preferred_element_type=jnp.float32)
    return jnp.concatenate([handed.astype(jnp.bfloat16), turned[MOVE:]], axis=0)


def solution(mesh):
    return jax.shard_map(
        local,
        mesh=mesh,
        in_specs=(
            P("wide", "narrow", None),
            P("wide", "narrow", None),
            P("wide", None),
            P("wide"),
            P("wide"),
            P("wide"),
        ),
        out_specs=P("wide", "narrow", None),
        check_vma=False,
    )
```

profile of v0, /device:TPU:0, one launch (start us, length us, event | category | flops | bytes accessed | tf_op | source)
XLA Modules:
  0.0 159.1 jit_solution(16922846225972821404)
XLA Ops:
  6.5 1.0 fusion.17
  7.6 0.7 broadcast_compare_fusion
  8.3 3.5 %fusion.12 = f32[32,256,256]{2,1,0:T(8,128)S(1)} fusion(bf16[32,64,256]{2,1,0:T(8,128)(2,1)S(1)} %copy-done, bf16[32,64,256]{2,1,0:T(8,128)(2,1)} %param.6, f32[32,256]{1,0:T(8,128)S(1)} %fusion.17, pred[32,64]{1,0:T(8,128)(4,1)S(1)} %broadcast_compare_fusion), kind=kOutput, calls=%fused_computation.21 | convolution fusion | flops 270532608 | bytes 10520576 | tf_op jit(solution)/shard_map/brd,bre->bde/dot_general | solution.py:35
  11.9 8.1 %fusion = f32[16,256,256]{2,0,1:T(8,128)S(1)} fusion(f32[32,256,256]{2,1,0:T(8,128)S(1)} %fusion.12, s32[32]{0:T(128)S(1)} %copy-done.3), kind=kOutput, calls=%fused_computation.1 | convolution fusion | flops 402653696 | bytes 12583040 | tf_op jit(solution)/shard_map/bl,bde->lde/dot_general | solution.py:37
  20.0 4.4 %copy.15 = f32[16,256,256]{2,1,0:T(8,128)} copy(f32[16,256,256]{2,0,1:T(8,128)S(1)} %fusion) | data formatting | bytes 8388608 | tf_op jit(solution)/shard_map/bl,bde->lde/dot_general | solution.py:37
  24.4 0.2 all-gather.3.cloned.1.call-start
  24.6 47.1 %reduce-scatter.2.cloned.1.call-done = f32[4,256,256]{2,1,0:T(8,128)} async-done(((f32[16,256,256]{2,1,0:T(8,128)}), f32[4,256,256]{2,1,0:T(8,128)}) %reduce-scatter.2.cloned.1.call-update) | async-done | bytes 1048592 | tf_op jit(solution)/shard_map/reduce_scatter | solution.py:36
  71.7 1.4 multiply_reduce_fusion
  73.1 2.9 %fusion.15 = f32[4,256,256]{2,1,0:T(8,128)S(1)} fusion(f32[4,256,256]{2,1,0:T(8,128)} %reduce-scatter.2.cloned.1.call-done, f32[4]{0:T(128)S(1)} %add_sqrt_fusion), kind=kOutput, calls=%fused_computation.25 | convolution fusion | flops 805568512 | bytes 2097168 | tf_op jit(solution)/shard_map/lde,lfe->ldf/dot_general | solution.py:17
  76.1 1.4 fusion.10
  77.4 1.2 fusion.26
  78.6 1.3 fusion.9
  79.9 1.2 fusion.27
  81.0 1.2 fusion.8
  82.3 1.2 fusion.28
  83.5 1.2 fusion.7
  84.7 1.2 fusion.29
  85.9 2.3 %fusion.11 = bf16[4,256,256]{2,1,0:T(8,128)(2,1)} fusion(f32[4,256,256]{2,1,0:T(8,128)S(1)} %fusion.29, f32[4,256,256]{2,1,0:T(8,128)S(1)} %fusion.7), kind=kOutput, calls=%fused_computation.18 | convolution fusion | flops 806354944 | bytes 2621440 | tf_op jit(solution)/shard_map/ldf,lfe->lde/dot_general | solution.py:18
  88.3 22.6 %all-gather.3.cloned.1.call-done = bf16[16,256,256]{2,1,0:T(8,128)(2,1)} async-done(((bf16[4,256,256]{2,1,0:T(8,128)(2,1)}), bf16[16,256,256]{2,1,0:T(8,128)(2,1)}) %all-gather.3.cloned.1.call-update) | async-done | bytes 2097168 | tf_op jit(solution)/shard_map/all_gather | solution.py:43
  110.9 3.1 %fusion.3 = bf16[32,256,256]{2,0,1:T(8,128)(2,1)S(1)} fusion(bf16[16,256,256]{2,1,0:T(8,128)(2,1)} %all-gather.3.cloned.1.call-done, s32[32]{0:T(128)S(1)} %copy-done.3), kind=kOutput, calls=%fused_computation.4 | convolution fusion | flops 67109376 | bytes 6291584 | tf_op jit(solution)/shard_map/bl,lde->bde/dot_general | solution.py:44
  114.0 5.2 %fusion.5 = bf16[32,64,256]{2,1,0:T(8,128)(2,1)S(1)} fusion(bf16[32,256,256]{2,0,1:T(8,128)(2,1)S(1)} %fusion.3, bf16[32,64,256]{2,1,0:T(8,128)(2,1)S(1)} %copy-done.1, f32[32,256]{1,0:T(8,128)S(1)} %fusion.17, pred[32,64]{1,0:T(8,128)(4,1)S(1)} %broadcast_compare_fusion), kind=kOutput, calls=%fused_computation.7 | convolution fusion | flops 271056896 | bytes 6326272 | tf_op jit(solution)/shard_map/brd,bde->bre/dot_general | solution.py:50
  119.4 31.5 %all-gather = bf16[16,64,256]{2,1,0:T(8,128)(2,1)S(1)} all-gather(bf16[2,64,256]{2,1,0:T(8,128)(2,1)S(1)} %slice.12), channel_id=2, replica_groups=mesh['wide'=8,'narrow'=4] {'wide'}, dimensions={0}, use_global_device_ids=true | all-gather | bytes 589824 | tf_op jit(solution)/shard_map/all_gather | solution.py:54
  150.8 0.4 fusion.13
  151.2 1.1 pad_maximum_fusion
  (20 shorter events, 0.2 us)
Async XLA Ops:
  6.5 1.8 %copy-start = (bf16[32,64,256]{2,1,0:T(8,128)(2,1)S(1)}, bf16[32,64,256]{2,1,0:T(8,128)(2,1)}, u32[]{:S(2)}) copy-start(bf16[32,64,256]{2,1,0:T(8,128)(2,1)} %param.7) | copy-start | bytes 3145732
  6.5 65.2 %reduce-scatter.2.cloned.1.call-start = ((), (), s32[]{:S(2)}) async-start(), calls=%async_computation.1 | async-start | bytes 5242880 | tf_op jit(solution)/shard_map/reduce_scatter | solution.py:36
  8.3 3.6 %copy-start.3 = (s32[32]{0:T(128)S(1)}, s32[32]{0:T(128)}, u32[]{:S(2)}) copy-start(s32[32]{0:T(128)} %param.9) | copy-start | bytes 388
  24.4 86.6 %all-gather.3.cloned.1.call-start = ((), (), s32[]{:S(2)}) async-start(), calls=%async_computation.2 | async-start | bytes 2621440 | tf_op jit(solution)/shard_map/all_gather | solution.py:43
  73.1 2.9 %copy-start.2 = (f32[4,256,256]{2,1,0:T(8,128)S(1)}, f32[4,256,256]{2,1,0:T(8,128)}, u32[]{:S(2)}) copy-start(f32[4,256,256]{2,1,0:T(8,128)} %reduce-scatter.2.cloned.1.call-done) | copy-start | bytes 3145732
  85.9 2.3 %copy-start.4 = (s32[32]{0:T(128)S(1)}, s32[32]{0:T(128)}, u32[]{:S(2)}) copy-start(s32[32]{0:T(128)} %param.11) | copy-start | bytes 388
  88.3 25.7 %copy-start.1 = (bf16[32,64,256]{2,1,0:T(8,128)(2,1)S(1)}, bf16[32,64,256]{2,1,0:T(8,128)(2,1)}, u32[]{:S(2)}) copy-start(bf16[32,64,256]{2,1,0:T(8,128)(2,1)} %param.6) | copy-start | bytes 3145732
Sparse Core Ops, SparseCore 0:
  24.5 47.1 reduce-scatter.1
  88.3 22.5 all-gather.2
where the time goes:
time: 159 us
  waiting for transfers between devices  69.8 us (44%)
  matrix products  36.3 us (23%)
  blocking collectives  31.5 us (20%)
  between operations  13.6 us (9%)
  local copies, waits for them, and re-layouts  4.46 us (3%)
  other arithmetic  3.3 us (2%)
    reduce_scatter x1, waiting for transfers between devices, local(): lax.psum_scatter(jnp.einsum('bl,bde->lde', list_pick, block_grams, precis...  47.1 us
    all_gather x1, blocking collectives, local(): part_rows = lax.all_gather(turned[None, :MOVE], 'wide', axis=0, tiled=True)  31.5 us
    all_gather x1, waiting for transfers between devices, local(): all_rotations = lax.all_gather(rotation, 'narrow', axis=0, tiled=True)  22.6 us
    dot_general x1, matrix products, local(): jnp.einsum('bl,bde->lde', list_pick, block_grams, precision=highest_prec)  8.11 us
    dot_general x5, matrix products, newton_polar(): jnp.einsum('lde,lfe->ldf', polar_iter, polar_iter, precision=highest_prec)  7.56 us
    dot_general x5, matrix products, newton_polar(): jnp.einsum('ldf,lfe->lde', product, polar_iter, precision=highest_prec)  7.36 us
    dot_general x1, matrix products, local(): jnp.einsum('brd,bde->bre', residual, chosen, preferred_element_type=jnp.f...  5.24 us
    dot_general x1, local copies, waits for them, and re-layouts, local(): jnp.einsum('bl,bde->lde', list_pick, block_grams, precision=highest_prec)  4.36 us
  transfers between devices with their start and end apart: 2, of which 2 were waited for; matrix products, arithmetic and copies ran while one was open for 0% of the time, Pallas kernels for 0%

commit v1 on v0

v1 whole, which is shorter than its diff:
```python
import functools

import jax
import jax.numpy as jnp
from jax import lax
from jax.experimental import pallas as pl
from jax.experimental.pallas import tpu as pltpu
from jax.sharding import PartitionSpec as P

MOVE = 2
ITERS = 5
CORES = 2
VMEM_LIMIT = 48 * 1024 * 1024

f32, bf16, i32 = jnp.float32, jnp.bfloat16, jnp.int32


def assign_slots(bl, ln, first_rows, slot_of_list, plan):
    blocks, lists = bl.shape[0], slot_of_list.shape[0]

    @pl.loop(0, lists)
    def _(l):
        slot_of_list[l] = -1

    def visit(b, nxt, wanted):
        l = bl[b]
        s = slot_of_list[l]
        new = jnp.logical_and(s < 0, wanted)
        slot_of_list[l] = jnp.where(new, nxt, s)
        return nxt + new.astype(i32)

    nxt = jnp.int32(0)
    for b in range(MOVE):
        nxt = visit(b, nxt, True)
    nxt = lax.fori_loop(MOVE, blocks, lambda b, n: visit(b, n, ln[b] > first_rows), nxt, unroll=True)
    plan[blocks] = nxt
    nxt = lax.fori_loop(MOVE, blocks, lambda b, n: visit(b, n, True), nxt, unroll=True)
    for b in range(blocks):
        plan[b] = slot_of_list[bl[b]]


def masked_residual(points, centroid_row, limit):
    rows = lax.broadcasted_iota(i32, points.shape, 0)
    return jnp.where(rows < limit, points.astype(f32) - centroid_row, 0.0).astype(bf16)


def gram_kernel(bl, ln, points, targets, centroids, plan, keep, send, slot_of_list, acc):
    blocks, rows, _ = points.shape
    me = lax.axis_index("narrow")
    core = lax.rem(me, CORES)
    assign_slots(bl, ln, CORES * rows, slot_of_list, plan)
    acc[...] = jnp.zeros_like(acc)

    @pl.loop(0, blocks, unroll=4)
    def _(b):
        slot = plan[b]
        residual = masked_residual(points[b], centroids[pl.ds(bl[b], 1), :], ln[b] - me * rows)
        acc[slot] += lax.dot_general(residual, targets[b], (((0,), (0,)), ((), ())), preferred_element_type=f32)

    @pl.loop(0, keep.shape[0])
    def _(i):
        keep[i] = acc[CORES * i + core]
        send[i] = acc[CORES * i + 1 - core].astype(bf16)


def newton_kernel(count, first, extra, keep, recv, *refs):
    extras, out = refs[:extra], refs[extra]
    xs = []
    for i in range(count):
        g = keep[i] + recv[i].astype(f32)
        for e in extras:
            g = g + e[i].astype(f32)
        xs.append(g * lax.rsqrt(jnp.sum(g * g) + 1e-6))
    for _ in range(ITERS):
        for i in range(count):
            x = xs[i]
            xb = x.astype(bf16)
            p = lax.dot_general(xb, xb, (((1,), (1,)), ((), ())), preferred_element_type=f32).astype(bf16)
            xs[i] = 1.5 * x - 0.5 * jnp.dot(p, xb, preferred_element_type=f32)
    for i in range(count):
        out[i] = xs[i].astype(bf16)


def newton(keep, recv, extras, first, count):
    shape = (count,) + keep.shape[1:]
    flops = count * ITERS * 4 * keep.shape[1] ** 3
    del first
    return pl.pallas_call(
        functools.partial(newton_kernel, count, 0, len(extras)),
        out_shape=jax.ShapeDtypeStruct(shape, bf16),
        in_specs=[pl.BlockSpec(memory_space=pltpu.VMEM)] * (2 + len(extras)),
        out_specs=pl.BlockSpec(memory_space=pltpu.VMEM),
        compiler_params=pltpu.CompilerParams(vmem_limit_bytes=VMEM_LIMIT),
        cost_estimate=pl.CostEstimate(flops=flops, bytes_accessed=count * 10 * 65536, transcendentals=0),
        name="newton",
    )(keep, recv, *extras)


def first_turn_kernel(bl, ln, plan, points, centroids, own, sibling, out):
    _, rows, _ = points.shape
    me = lax.axis_index("narrow")
    core = lax.rem(me, CORES)
    for b in range(MOVE):
        mine = lax.rem(plan[b], CORES) == core
        residual = masked_residual(points[b], centroids[pl.ds(bl[b], 1), :], ln[b] - me * rows)
        rotation = jnp.where(mine, own[0], sibling[0])
        out[b] = jnp.dot(residual, rotation, preferred_element_type=f32).astype(bf16)


def turn_kernel(starts, n_parts, bl, ln, plan, points, centroids, *refs):
    owns, siblings = refs[:n_parts], refs[n_parts:2 * n_parts]
    out, rots = refs[2 * n_parts:]
    blocks, rows, _ = points.shape
    me = lax.axis_index("narrow")
    core = lax.rem(me, CORES)
    for s, o, t in zip(starts, owns, siblings):
        for i in range(o.shape[0]):
            rots[CORES * (s + i) + core] = o[i]
            rots[CORES * (s + i) + 1 - core] = t[i]

    @pl.loop(MOVE, blocks, unroll=6)
    def _(b):
        residual = masked_residual(points[b], centroids[pl.ds(bl[b], 1), :], ln[b] - me * rows)
        out[b] = jnp.dot(residual, rots[plan[b]], preferred_element_type=f32).astype(bf16)


def chunk_sizes(per, capped):
    cap = per * 3 // 4 if capped else per
    sizes, left = [1], cap - 1
    while left > 1:
        sizes.append(min(2, left - 1))
        left -= sizes[-1]
    if left:
        sizes.append(left)
    return sizes, cap


def local(wide, narrow, points, targets, centroids, block_list, lengths, sources):
    blocks, rows, width = points.shape
    lists = centroids.shape[0]
    per = lists // CORES
    chips = narrow // CORES
    smem, vmem = pl.BlockSpec(memory_space=pltpu.SMEM), pl.BlockSpec(memory_space=pltpu.VMEM)
    params = pltpu.CompilerParams(vmem_limit_bytes=VMEM_LIMIT)
    mat = (width, width)

    plan, keep, send = pl.pallas_call(
        gram_kernel,
        out_shape=(
            jax.ShapeDtypeStruct((blocks + 1,), i32),
            jax.ShapeDtypeStruct((per,) + mat, f32),
            jax.ShapeDtypeStruct((per,) + mat, bf16),
        ),
        in_specs=[smem, smem, vmem, vmem, vmem],
        out_specs=(smem, vmem, vmem),
        scratch_shapes=[pltpu.SMEM((lists,), i32), pltpu.VMEM((lists,) + mat, f32)],
        compiler_params=params,
        cost_estimate=pl.CostEstimate(flops=2 * blocks * rows * width * width, bytes_accessed=6 << 20, transcendentals=0),
        name="grams",
    )(block_list, lengths, points, targets, centroids)

    to_core = [(i, i ^ 1) for i in range(narrow)]
    to_chip = [[(i, (i + CORES * k) % narrow) for i in range(narrow)] for k in range(1, chips)]

    sizes, cap = chunk_sizes(per, chips == 2)
    starts = [sum(sizes[:i]) for i in range(len(sizes))]
    bounds = list(zip(starts, sizes))
    all_bounds = bounds + ([(cap, per - cap)] if cap < per else [])

    recvs, chip_sums = [], []
    for s, n in all_bounds:
        recv = lax.ppermute(send[s:s + n], "narrow", to_core)
        recvs.append(recv)
        chip_sums.append((keep[s:s + n] + recv.astype(f32)).astype(bf16))

    def cross(part):
        return tuple(lax.ppermute(part, "narrow", perm) for perm in to_chip)

    crossed = [cross(part) for part in chip_sums[:len(bounds)]]
    if cap < per:
        rest = chip_sums[-1]
        crossed.append(
            lax.cond(plan[blocks] > CORES * cap, cross, lambda part: tuple(jnp.zeros_like(part) for _ in to_chip), rest)
        )

    owns, siblings = [], []
    for (s, n), recv, extras in zip(all_bounds, recvs, crossed):
        own = newton(keep[s:s + n], recv, extras, s, n)
        owns.append(own)
        siblings.append(lax.ppermute(own, "narrow", to_core))

    leading = pl.pallas_call(
        first_turn_kernel,
        out_shape=jax.ShapeDtypeStruct((MOVE, rows, width), bf16),
        in_specs=[smem, smem, smem] + [vmem] * 4,
        out_specs=vmem,
        compiler_params=params,
        cost_estimate=pl.CostEstimate(flops=2 * MOVE * rows * width * width, bytes_accessed=1 << 19, transcendentals=0),
        name="turn_leading",
    )(block_list, lengths, plan, points[:MOVE], centroids, owns[0], siblings[0])

    donors = sources[:MOVE] // blocks
    if wide <= 16 and wide & (wide - 1) == 0:
        here = lax.axis_index("wide")
        parts = [leading] + [lax.ppermute(leading, "wide", [(i, i ^ k) for i in range(wide)]) for k in range(1, wide)]
        hops = jnp.bitwise_xor(donors, here)
    else:
        gathered = lax.all_gather(leading, "wide", axis=0)
        parts = [gathered[k] for k in range(wide)]
        hops = donors
    handed = parts[0]
    for k in range(1, wide):
        handed = jnp.where((hops == k)[:, None, None], parts[k], handed)

    turned = pl.pallas_call(
        functools.partial(turn_kernel, [s for s, _ in all_bounds], len(owns)),
        out_shape=jax.ShapeDtypeStruct((blocks, rows, width), bf16),
        in_specs=[smem, smem, smem] + [vmem] * (2 + 2 * len(owns)),
        out_specs=vmem,
        scratch_shapes=[pltpu.VMEM((lists,) + mat, bf16)],
        compiler_params=params,
        cost_estimate=pl.CostEstimate(flops=2 * blocks * rows * width * width, bytes_accessed=4 << 20, transcendentals=0),
        name="turn",
    )(block_list, lengths, plan, points, centroids, *owns, *siblings)
    return lax.dynamic_update_slice(turned, handed, (0, 0, 0))


def solution(mesh):
    return jax.shard_map(
        functools.partial(local, mesh.shape["wide"], mesh.shape["narrow"]),
        mesh=mesh,
        in_specs=(
            P("wide", "narrow", None),
            P("wide", "narrow", None),
            P("wide", None),
            P("wide"),
            P("wide"),
            P("wide"),
        ),
        out_specs=P("wide", "narrow", None),
        check_vma=False,
    )
```

time: 159 us -> 66.5 us (0.42)
  waiting for transfers between devices: 69.8 us -> 9.8 us
  matrix products: 36.3 us -> 0 us
  blocking collectives: 31.5 us -> 0 us
  Pallas kernels: 0 us -> 22.6 us
  starting transfers between devices: 0.22 us -> 22.3 us
  between operations: 13.6 us -> 0.81 us
  local copies, waits for them, and re-layouts: 4.46 us -> 7.91 us
    reduce_scatter x1 -> x0, waiting for transfers between devices: 47.1 us -> none  [local(): lax.psum_scatter(jnp.einsum('bl,bde->lde', list_pick, block_grams, precis...]
    dot_general x16 -> x0, matrix products: 36.3 us -> none  [the longest x1 8.11 us: local(): jnp.einsum('bl,bde->lde', list_pick, block_grams, precision=highest_prec)]
    all_gather x1 -> x0, blocking collectives: 31.5 us -> none  [local(): part_rows = lax.all_gather(turned[None, :MOVE], 'wide', axis=0, tiled=True)]
    all_gather x1 -> x0, waiting for transfers between devices: 22.6 us -> none  [local(): all_rotations = lax.all_gather(rotation, 'narrow', axis=0, tiled=True)]
    pallas_call x0 -> x8, Pallas kernels: none -> 22.6 us  [the longest x5 13.6 us: newton(): pl.pallas_call(functools.partial(newton_kernel, count, 0, len(extras)), o...]
    ppermute x0 -> x21, starting transfers between devices: none -> 22.3 us  [the longest x7 14.4 us: local(): lax.ppermute(leading, 'wide', [(i, i ^ k) for i in range(wide)])]
    ppermute x0 -> x21, waiting for transfers between devices: none -> 9.8 us  [the longest x4 7.45 us: cross(): return tuple((lax.ppermute(part, 'narrow', perm) for perm in to_chip))]
    unnamed x10 -> x22, local copies, waits for them, and re-layouts: 0.02 us -> 6.46 us
  transfers between devices with their start and end apart: 2 -> 21, of which waited for: 2 -> 6; matrix products, arithmetic and copies ran while one was open for 0% -> 5% of each run, Pallas kernels for 0% -> 27%
where the time goes in v1:
time: 66.5 us; the launch traced here: 66.1 us
  Pallas kernels  22.6 us (34%)
  starting transfers between devices  22.3 us (34%)
  waiting for transfers between devices  9.8 us (15%)
  local copies, waits for them, and re-layouts  7.91 us (12%)
  other arithmetic  2.58 us (4%)
  between operations  0.81 us (1%)
    ppermute x7, starting transfers between devices, local(): lax.ppermute(leading, 'wide', [(i, i ^ k) for i in range(wide)])  14.4 us
    pallas_call x5, Pallas kernels, newton(): pl.pallas_call(functools.partial(newton_kernel, count, 0, len(extras)), o...  13.6 us
    ppermute x4, waiting for transfers between devices, cross(): return tuple((lax.ppermute(part, 'narrow', perm) for perm in to_chip))  7.45 us
    unnamed x22, local copies, waits for them, and re-layouts  6.46 us
    ppermute x4, starting transfers between devices, cross(): return tuple((lax.ppermute(part, 'narrow', perm) for perm in to_chip))  5.02 us
    pallas_call x1, Pallas kernels, local(): pl.pallas_call(gram_kernel, out_shape=(jax.ShapeDtypeStruct((blocks + 1,)...  4.81 us
    pallas_call x1, Pallas kernels, local(): pl.pallas_call(functools.partial(turn_kernel, [s for s, _ in all_bounds],...  3.46 us
    ppermute x5, starting transfers between devices, local(): recv = lax.ppermute(send[s:s + n], 'narrow', to_core)  1.61 us
  transfers between devices with their start and end apart: 21, of which 6 were waited for; matrix products, arithmetic and copies ran while one was open for 5% of the time, Pallas kernels for 27%

profile of v1, /device:TPU:0, one launch (start us, length us, event | category | flops | bytes accessed | tf_op | source)
XLA Modules:
  0.0 66.1 jit_solution(13371555738450927829)
XLA Ops:
  0.0 1.2 %copy-done = bf16[32,64,256]{2,1,0:T(8,128)(2,1)S(1)} copy-done((bf16[32,64,256]{2,1,0:T(8,128)(2,1)S(1)}, bf16[32,64,256]{2,1,0:T(8,128)(2,1)}, u32[]{:S(2)}) %copy-start) | copy-done | bytes 1048600
  1.2 1.2 %copy-done.2 = bf16[32,64,256]{2,1,0:T(8,128)(2,1)S(1)} copy-done((bf16[32,64,256]{2,1,0:T(8,128)(2,1)S(1)}, bf16[32,64,256]{2,1,0:T(8,128)(2,1)}, u32[]{:S(2)}) %copy-start.2) | copy-done | bytes 1048600
  2.5 0.7 %copy-done.3 = f32[16,256]{1,0:T(8,128)S(1)} copy-done((f32[16,256]{1,0:T(8,128)S(1)}, f32[16,256]{1,0:T(8,128)}, u32[]{:S(2)}) %copy-start.3) | copy-done | bytes 16408
  4.5 4.8 %grams.1 = (s32[33]{0:T(128)S(1)}, f32[8,256,256]{2,1,0:T(8,128)S(1)}, bf16[8,256,256]{2,1,0:T(8,128)(2,1)S(1)}) custom-call(s32[32]{0:T(128)S(1)} %copy-done.5, s32[32]{0:T(128)S(1)} %copy-done.7, bf16[32,64,256]{2,1,0:T(8,128)(2,1)S(1)} %copy-done, bf16[32,64,256]{2,1,0:T(8,128)(2,1)S(1)} %copy-done.2, f32[16,256]{1,0:T(8,128)S(1)} %copy-done.3), custom_call_target="tpu_custom_call" | custom-call | flops 268435456 | bytes 6291456 | tf_op jit(solution)/shard_map/grams/pallas_call | solution.py:147
  11.8 1.1 %add_convert_fusion = (bf16[2,256,256]{2,1,0:T(8,128)(2,1)S(1)}, bf16[2,256,256]{2,1,0:T(8,128)(2,1)}, bf16[2,256,256]{2,1,0:T(8,128)(2,1)}, f32[2,256,256]{2,1,...) fusion(bf16[2,256,256]{2,1,0:T(8,128)(2,1)S(1)} %collective-permute-done.9.recv, ...), kind=kLoop, calls=%fused_computation | loop fusion | flops 1179648 | bytes 4718592 | tf_op jit(solution)/shard_map/convert_element_type | solution.py:174
  12.9 2.9 %collective-permute-start.4 = (bf16[2,256,256]{2,1,0:T(8,128)(2,1)}, bf16[2,256,256]{2,1,0:T(8,128)(2,1)}, u32[]{:S(2)}, u32[]{:S(2)}) collective-permute-start(bf16[2,256,256]{2,1,0:T(8,128)(2,1)} %get-tuple-element.18), channel_id=1, source_target_pairs={{0,2},{1,3},{2,0},{3,1},{4,6},{5,7},{6,4},{7,5},{8,10},{9,11},{10,... | collective-permute-start | bytes 786440 | tf_op jit(solution)/shard_map/ppermute | solution.py:177
  15.9 2.0 %collective-permute-start.8 = (bf16[1,256,256]{2,1,0:T(8,128)(2,1)S(1)}, bf16[1,256,256]{2,1,0:T(8,128)(2,1)S(1)}, u32[]{:S(2)}, u32[]{:S(2)}) collective-permute-start(bf16[1,256,256]{2,1,0:T(8,128)(2,1)S(1)} %get-tuple-element.23), channel_id=1, source_target_pairs={{0,2},{1,3},{2,0},{3,1},{4,6},{5,7},{6,4},{7,5},{8,10},{9,11},{10,... | collective-permute-start | bytes 393224 | tf_op jit(solution)/shard_map/ppermute | solution.py:177
  19.3 6.6 %collective-permute-done.2.refs_0_ = bf16[1,256,256]{2,1,0:T(8,128)(2,1)S(1)} collective-permute-done((bf16[1,256,256]{2,1,0:T(8,128)(2,1)S(1)}, bf16[1,256,256]{2,1,0:T(8,128)(2,1)S(1)}, u32[]{:S(2)}, u32[]{:S(2)}) %collective-permute-start.2) | collective-permute-done | bytes 131104 | tf_op jit(solution)/shard_map/ppermute | solution.py:177
  25.8 1.8 %newton.5.refs_0_.own = bf16[1,256,256]{2,1,0:T(8,128)(2,1)S(1)} custom-call(f32[1,256,256]{2,1,0:T(8,128)S(1)} %get-tuple-element.26.keep, bf16[1,256,256]{2,1,0:T(8,128)(2,1)S(1)} %collective-permute-done.1.recv, bf16[1,256,256]{2,1,0:T(8,128)(2,1)S(1)} %collective-permute-done.2.refs_0_), custom_call_target="tpu_custom_call" | custom-call | flops 335544320 | bytes 655360 | tf_op jit(solution)/shard_map/newton/pallas_call | solution.py:88
  27.8 0.9 %collective-permute-done.8.refs_0_ = bf16[1,256,256]{2,1,0:T(8,128)(2,1)S(1)} collective-permute-done((bf16[1,256,256]{2,1,0:T(8,128)(2,1)S(1)}, bf16[1,256,256]{2,1,0:T(8,128)(2,1)S(1)}, u32[]{:S(2)}, u32[]{:S(2)}) %collective-permute-start.8) | collective-permute-done | bytes 131104 | tf_op jit(solution)/shard_map/ppermute | solution.py:177
  28.6 1.8 %newton.8.refs_3_ = bf16[1,256,256]{2,1,0:T(8,128)(2,1)S(1)} custom-call(f32[1,256,256]{2,1,0:T(8,128)S(1)} %get-tuple-element.25.keep, bf16[1,256,256]{2,1,0:T(8,128)(2,1)S(1)} %collective-permute-done.7.recv, bf16[1,256,256]{2,1,0:T(8,128)(2,1)S(1)} %collective-permute-done.8.refs_0_), custom_call_target="tpu_custom_call" | custom-call | flops 335544320 | bytes 655360 | tf_op jit(solution)/shard_map/newton/pallas_call | solution.py:88
  30.6 0.7 %conditional.1 = (bf16[2,256,256]{2,1,0:T(8,128)(2,1)}) conditional(s32[]{:T(128)} %bitcast, () %tuple.11, bf16[2,256,256]{2,1,0:T(8,128)(2,1)S(1)} %get-tuple-element.17), branch_computations={%region_0.0_spmd, %region_1.0_spmd} | conditional | bytes 1048624 | solution.py:183
  30.6 0.7 %broadcast.32 = bf16[2,256,256]{2,1,0:T(8,128)(2,1)} broadcast(bf16[]{:T(256)} %constant.11.clone), dimensions={} | broadcast | bytes 262146 | tf_op jit(solution)/shard_map/broadcast.8
  31.3 3.0 %newton.9.refs_4_ = bf16[2,256,256]{2,1,0:T(8,128)(2,1)S(1)} custom-call(f32[2,256,256]{2,1,0:T(8,128)S(1)} %get-tuple-element.20.keep, bf16[2,256,256]{2,1,0:T(8,128)(2,1)S(1)} %collective-permute-done.9.recv, bf16[2,256,256]{2,1,0:T(8,128)(2,1)} %get-tuple-element.38.refs_0_), custom_call_target="tpu_custom_call" | custom-call | flops 671088640 | bytes 1310720 | tf_op jit(solution)/shard_map/newton/pallas_call | solution.py:88
  34.9 3.8 %newton.6.refs_1_ = bf16[2,256,256]{2,1,0:T(8,128)(2,1)} custom-call(f32[2,256,256]{2,1,0:T(8,128)S(1)} %get-tuple-element.22.keep, bf16[2,256,256]{2,1,0:T(8,128)(2,1)S(1)} %collective-permute-done.3.recv, bf16[2,256,256]{2,1,0:T(8,128)(2,1)} %collective-permute-done.4.refs_0_), custom_call_target="tpu_custom_call" | custom-call | flops 671088640 | bytes 1310720 | tf_op jit(solution)/shard_map/newton/pallas_call | solution.py:88
  38.8 3.0 %newton.7.refs_2_ = bf16[2,256,256]{2,1,0:T(8,128)(2,1)S(1)} custom-call(f32[2,256,256]{2,1,0:T(8,128)S(1)} %get-tuple-element.21.keep, bf16[2,256,256]{2,1,0:T(8,128)(2,1)S(1)} %collective-permute-done.5.recv, bf16[2,256,256]{2,1,0:T(8,128)(2,1)} %collective-permute-done.6.refs_0_), custom_call_target="tpu_custom_call" | custom-call | flops 671088640 | bytes 1310720 | tf_op jit(solution)/shard_map/newton/pallas_call | solution.py:88
  44.4 0.7 %turn_leading.1 = bf16[2,64,256]{2,1,0:T(8,128)(2,1)S(1)} custom-call(s32[32]{0:T(128)S(1)} %copy-done.6, s32[32]{0:T(128)S(1)} %copy-done.8, s32[33]{0:T(128)S(1)} %copy-done.10, bf16[2,64,256]{2,1,0:T(8,128)(2,1)S(1)} %slice.56.points, f32[16,256]{1,0:T(8,128)S(1)} %copy-done.4, bf16[1,256,256]{2,1,0:T(8,128)(2,1)S(1)} %newton.5.refs_0_.own, ...), custom_call_target="tpu_custom_call" | custom-call | flops 16777216 | bytes 524288 | tf_op jit(solution)/shard_map/turn_leading/pallas_call | solution.py:192
  45.1 5.2 %collective-permute-start.15 = (bf16[2,64,256]{2,1,0:T(8,128)(2,1)S(1)}, bf16[2,64,256]{2,1,0:T(8,128)(2,1)S(1)}, u32[]{:S(2)}, u32[]{:S(2)}) collective-permute-start(bf16[2,64,256]{2,1,0:T(8,128)(2,1)S(1)} %turn_leading.1), channel_id=1, source_target_pairs={{0,28},{4,24},{8,20},{12,16},{16,12},{20,8},{24,4},{28,0},{1,29},{... | collective-permute-start | bytes 196616 | tf_op jit(solution)/shard_map/ppermute | solution.py:205
  51.2 1.5 %collective-permute-done.15 = bf16[2,64,256]{2,1,0:T(8,128)(2,1)S(1)} collective-permute-done((bf16[2,64,256]{2,1,0:T(8,128)(2,1)S(1)}, bf16[2,64,256]{2,1,0:T(8,128)(2,1)S(1)}, u32[]{:S(2)}, u32[]{:S(2)}) %collective-permute-start.15) | collective-permute-done | bytes 65568 | tf_op jit(solution)/shard_map/ppermute | solution.py:205
  52.7 5.0 %collective-permute-start.17 = (bf16[2,64,256]{2,1,0:T(8,128)(2,1)S(1)}, bf16[2,64,256]{2,1,0:T(8,128)(2,1)S(1)}, u32[]{:S(2)}, u32[]{:S(2)}) collective-permute-start(bf16[2,64,256]{2,1,0:T(8,128)(2,1)S(1)} %turn_leading.1), channel_id=1, source_target_pairs={{0,20},{4,16},{8,28},{12,24},{16,4},{20,0},{24,12},{28,8},{1,21},{... | collective-permute-start | bytes 196616 | tf_op jit(solution)/shard_map/ppermute | solution.py:205
  58.5 1.8 %collective-permute-start.20 = (bf16[2,64,256]{2,1,0:T(8,128)(2,1)S(1)}, bf16[2,64,256]{2,1,0:T(8,128)(2,1)S(1)}, u32[]{:S(2)}, u32[]{:S(2)}) collective-permute-start(bf16[2,64,256]{2,1,0:T(8,128)(2,1)S(1)} %turn_leading.1), channel_id=1, source_target_pairs={{0,8},{4,12},{8,0},{12,4},{16,24},{20,28},{24,16},{28,20},{1,9},{5... | collective-permute-start | bytes 196616 | tf_op jit(solution)/shard_map/ppermute | solution.py:205
  60.2 1.5 %collective-permute-start.21 = (bf16[2,64,256]{2,1,0:T(8,128)(2,1)S(1)}, bf16[2,64,256]{2,1,0:T(8,128)(2,1)S(1)}, u32[]{:S(2)}, u32[]{:S(2)}) collective-permute-start(bf16[2,64,256]{2,1,0:T(8,128)(2,1)S(1)} %turn_leading.1), channel_id=1, source_target_pairs={{0,4},{4,0},{8,12},{12,8},{16,20},{20,16},{24,28},{28,24},{1,5},{5... | collective-permute-start | bytes 196616 | tf_op jit(solution)/shard_map/ppermute | solution.py:205
  61.8 3.5 %turn.1 = bf16[32,64,256]{2,1,0:T(8,128)(2,1)} custom-call(s32[32]{0:T(128)S(1)} %copy-done.6, s32[32]{0:T(128)S(1)} %copy-done.8, s32[33]{0:T(128)S(1)} %copy-done.10, bf16[32,64,256]{2,1,0:T(8,128)(2,1)S(1)} %copy-done.1, f32[16,256]{1,0:T(8,128)S(1)} %copy-done.4, bf16[1,256,256]{2,1,0:T(8,128)(2,1)S(1)} %newton.5.refs_0_.own, ...), custom_call_target="tpu_custom_call" | custom-call | flops 268435456 | bytes 4194304 | tf_op jit(solution)/shard_map/turn/pallas_call | solution.py:215
  65.3 0.8 %select_dynamic-update-slice_fusion = bf16[32,64,256]{2,1,0:T(8,128)(2,1)} fusion(bf16[32,64,256]{2,1,0:T(8,128)(2,1)} %turn.1, bf16[2,64,256]{2,1,0:T(8,128)(2,1)S(1)} %collective-permute-done.15, bf16[2,64,256]{2,1,0:T(8,128)(2,1)S(1)} %collective-permute-done.16, bf16[2,64,256]{2,1,0:T(8,128)(2,1)S(1)} %collective-permute-done.17, ...), kind=kLoop, calls=%fused_computation.5 | loop fusion | flops 229376 | bytes 589838 | tf_op jit(solution)/shard_map/dynamic_update_slice | solution.py:225
  (59 shorter events, 9.5 us)
Async XLA Ops:
  9.3 8.7 %copy-start.9 = (s32[33]{0:T(128)}, s32[33]{0:T(128)S(1)}, u32[]{:S(2)}) copy-start(s32[33]{0:T(128)S(1)} %get-tuple-element.12.plan) | copy-start | bytes 400
  9.4 1.7 %collective-permute-start.9 = (bf16[2,256,256]{2,1,0:T(8,128)(2,1)S(1)}, bf16[2,256,256]{2,1,0:T(8,128)(2,1)S(1)}, u32[]{:S(2)}, u32[]{:S(2)}) collective-permute-start(bf16[2,256,256]{2,1,0:T(8,128)(2,1)S(1)} %get-tuple-element.27), channel_id=1, source_target_pairs={{0,1},{1,0},{2,3},{3,2},{4,5},{5,4},{6,7},{7,6},{8,9},{9,8},{10,11... | collective-permute-start | bytes 786440 | tf_op jit(solution)/shard_map/ppermute | solution.py:172
  9.9 1.5 %collective-permute-start.3 = (bf16[2,256,256]{2,1,0:T(8,128)(2,1)S(1)}, bf16[2,256,256]{2,1,0:T(8,128)(2,1)S(1)}, u32[]{:S(2)}, u32[]{:S(2)}) collective-permute-start(bf16[2,256,256]{2,1,0:T(8,128)(2,1)S(1)} %get-tuple-element.29), channel_id=1, source_target_pairs={{0,1},{1,0},{2,3},{3,2},{4,5},{5,4},{6,7},{7,6},{8,9},{9,8},{10,11... | collective-permute-start | bytes 786440 | tf_op jit(solution)/shard_map/ppermute | solution.py:172
  10.0 1.8 %collective-permute-start.5 = (bf16[2,256,256]{2,1,0:T(8,128)(2,1)S(1)}, bf16[2,256,256]{2,1,0:T(8,128)(2,1)S(1)}, u32[]{:S(2)}, u32[]{:S(2)}) collective-permute-start(bf16[2,256,256]{2,1,0:T(8,128)(2,1)S(1)} %get-tuple-element.28), channel_id=1, source_target_pairs={{0,1},{1,0},{2,3},{3,2},{4,5},{5,4},{6,7},{7,6},{8,9},{9,8},{10,11... | collective-permute-start | bytes 786440 | tf_op jit(solution)/shard_map/ppermute | solution.py:172
  10.4 5.3 %collective-permute-start.7 = (bf16[1,256,256]{2,1,0:T(8,128)(2,1)S(1)}, bf16[1,256,256]{2,1,0:T(8,128)(2,1)S(1)}, u32[]{:S(2)}, u32[]{:S(2)}) collective-permute-start(bf16[1,256,256]{2,1,0:T(8,128)(2,1)S(1)} %get-tuple-element.30), channel_id=1, source_target_pairs={{0,1},{1,0},{2,3},{3,2},{4,5},{5,4},{6,7},{7,6},{8,9},{9,8},{10,11... | collective-permute-start | bytes 393224 | tf_op jit(solution)/shard_map/ppermute | solution.py:172
  10.6 5.2 %collective-permute-start.1 = (bf16[1,256,256]{2,1,0:T(8,128)(2,1)S(1)}, bf16[1,256,256]{2,1,0:T(8,128)(2,1)S(1)}, u32[]{:S(2)}, u32[]{:S(2)}) collective-permute-start(bf16[1,256,256]{2,1,0:T(8,128)(2,1)S(1)} %get-tuple-element.31), channel_id=1, source_target_pairs={{0,1},{1,0},{2,3},{3,2},{4,5},{5,4},{6,7},{7,6},{8,9},{9,8},{10,11... | collective-permute-start | bytes 393224 | tf_op jit(solution)/shard_map/ppermute | solution.py:172
  12.9 22.0 %collective-permute-start.4 = (bf16[2,256,256]{2,1,0:T(8,128)(2,1)}, bf16[2,256,256]{2,1,0:T(8,128)(2,1)}, u32[]{:S(2)}, u32[]{:S(2)}) collective-permute-start(bf16[2,256,256]{2,1,0:T(8,128)(2,1)} %get-tuple-element.18), channel_id=1, source_target_pairs={{0,2},{1,3},{2,0},{3,1},{4,6},{5,7},{6,4},{7,5},{8,10},{9,11},{10,... | collective-permute-start | bytes 786440 | tf_op jit(solution)/shard_map/ppermute | solution.py:177
  15.8 10.0 %collective-permute-start.2 = (bf16[1,256,256]{2,1,0:T(8,128)(2,1)S(1)}, bf16[1,256,256]{2,1,0:T(8,128)(2,1)S(1)}, u32[]{:S(2)}, u32[]{:S(2)}) collective-permute-start(bf16[1,256,256]{2,1,0:T(8,128)(2,1)S(1)} %get-tuple-element.24), channel_id=1, source_target_pairs={{0,2},{1,3},{2,0},{3,1},{4,6},{5,7},{6,4},{7,5},{8,10},{9,11},{10,... | collective-permute-start | bytes 393224 | tf_op jit(solution)/shard_map/ppermute | solution.py:177
  15.9 12.7 %collective-permute-start.8 = (bf16[1,256,256]{2,1,0:T(8,128)(2,1)S(1)}, bf16[1,256,256]{2,1,0:T(8,128)(2,1)S(1)}, u32[]{:S(2)}, u32[]{:S(2)}) collective-permute-start(bf16[1,256,256]{2,1,0:T(8,128)(2,1)S(1)} %get-tuple-element.23), channel_id=1, source_target_pairs={{0,2},{1,3},{2,0},{3,1},{4,6},{5,7},{6,4},{7,5},{8,10},{9,11},{10,... | collective-permute-start | bytes 393224 | tf_op jit(solution)/shard_map/ppermute | solution.py:177
  17.9 20.9 %collective-permute-start.6 = (bf16[2,256,256]{2,1,0:T(8,128)(2,1)}, bf16[2,256,256]{2,1,0:T(8,128)(2,1)}, u32[]{:S(2)}, u32[]{:S(2)}) collective-permute-start(bf16[2,256,256]{2,1,0:T(8,128)(2,1)} %get-tuple-element.19), channel_id=1, source_target_pairs={{0,2},{1,3},{2,0},{3,1},{4,6},{5,7},{6,4},{7,5},{8,10},{9,11},{10,... | collective-permute-start | bytes 786440 | tf_op jit(solution)/shard_map/ppermute | solution.py:177
  27.7 14.7 %collective-permute-start.10 = (bf16[1,256,256]{2,1,0:T(8,128)(2,1)S(1)}, bf16[1,256,256]{2,1,0:T(8,128)(2,1)S(1)}, u32[]{:S(2)}, u32[]{:S(2)}) collective-permute-start(bf16[1,256,256]{2,1,0:T(8,128)(2,1)S(1)} %newton.5.refs_0_.own), channel_id=1, source_target_pairs={{0,1},{1,0},{2,3},{3,2},{4,5},{5,4},{6,7},{7,6},{8,9},{9,8},{10,11... | collective-permute-start | bytes 393224 | tf_op jit(solution)/shard_map/ppermute | solution.py:190
  30.5 19.8 %collective-permute-start.13 = (bf16[1,256,256]{2,1,0:T(8,128)(2,1)S(1)}, bf16[1,256,256]{2,1,0:T(8,128)(2,1)}, u32[]{:S(2)}, u32[]{:S(2)}) collective-permute-start(bf16[1,256,256]{2,1,0:T(8,128)(2,1)S(1)} %newton.8.refs_3_), channel_id=1, source_target_pairs={{0,1},{1,0},{2,3},{3,2},{4,5},{5,4},{6,7},{7,6},{8,9},{9,8},{10,11... | collective-permute-start | bytes 393224 | tf_op jit(solution)/shard_map/ppermute | solution.py:190
  34.4 23.9 %collective-permute-start.14 = (bf16[2,256,256]{2,1,0:T(8,128)(2,1)S(1)}, bf16[2,256,256]{2,1,0:T(8,128)(2,1)S(1)}, u32[]{:S(2)}, u32[]{:S(2)}) collective-permute-start(bf16[2,256,256]{2,1,0:T(8,128)(2,1)S(1)} %newton.9.refs_4_), channel_id=1, source_target_pairs={{0,1},{1,0},{2,3},{3,2},{4,5},{5,4},{6,7},{7,6},{8,9},{9,8},{10,11... | collective-permute-start | bytes 786440 | tf_op jit(solution)/shard_map/ppermute | solution.py:190
  34.9 7.5 %copy-start.1 = (bf16[32,64,256]{2,1,0:T(8,128)(2,1)S(1)}, bf16[32,64,256]{2,1,0:T(8,128)(2,1)}, u32[]{:S(2)}) copy-start(bf16[32,64,256]{2,1,0:T(8,128)(2,1)} %points.3) | copy-start | bytes 3145732
  34.9 7.5 %copy-start.4 = (f32[16,256]{1,0:T(8,128)S(1)}, f32[16,256]{1,0:T(8,128)}, u32[]{:S(2)}) copy-start(f32[16,256]{1,0:T(8,128)} %centroids.5) | copy-start | bytes 49156
  38.7 19.7 %collective-permute-start.11 = (bf16[2,256,256]{2,1,0:T(8,128)(2,1)}, bf16[2,256,256]{2,1,0:T(8,128)(2,1)S(1)}, u32[]{:S(2)}, u32[]{:S(2)}) collective-permute-start(bf16[2,256,256]{2,1,0:T(8,128)(2,1)} %newton.6.refs_1_), channel_id=1, source_target_pairs={{0,1},{1,0},{2,3},{3,2},{4,5},{5,4},{6,7},{7,6},{8,9},{9,8},{10,11... | collective-permute-start | bytes 786440 | tf_op jit(solution)/shard_map/ppermute | solution.py:190
  41.8 18.4 %collective-permute-start.12 = (bf16[2,256,256]{2,1,0:T(8,128)(2,1)S(1)}, bf16[2,256,256]{2,1,0:T(8,128)(2,1)S(1)}, u32[]{:S(2)}, u32[]{:S(2)}) collective-permute-start(bf16[2,256,256]{2,1,0:T(8,128)(2,1)S(1)} %newton.7.refs_2_), channel_id=1, source_target_pairs={{0,1},{1,0},{2,3},{3,2},{4,5},{5,4},{6,7},{7,6},{8,9},{9,8},{10,11... | collective-permute-start | bytes 786440 | tf_op jit(solution)/shard_map/ppermute | solution.py:190
  45.1 7.6 %collective-permute-start.15 = (bf16[2,64,256]{2,1,0:T(8,128)(2,1)S(1)}, bf16[2,64,256]{2,1,0:T(8,128)(2,1)S(1)}, u32[]{:S(2)}, u32[]{:S(2)}) collective-permute-start(bf16[2,64,256]{2,1,0:T(8,128)(2,1)S(1)} %turn_leading.1), channel_id=1, source_target_pairs={{0,28},{4,24},{8,20},{12,16},{16,12},{20,8},{24,4},{28,0},{1,29},{... | collective-permute-start | bytes 196616 | tf_op jit(solution)/shard_map/ppermute | solution.py:205
  50.3 7.4 %collective-permute-start.16 = (bf16[2,64,256]{2,1,0:T(8,128)(2,1)S(1)}, bf16[2,64,256]{2,1,0:T(8,128)(2,1)S(1)}, u32[]{:S(2)}, u32[]{:S(2)}) collective-permute-start(bf16[2,64,256]{2,1,0:T(8,128)(2,1)S(1)} %turn_leading.1), channel_id=1, source_target_pairs={{0,24},{4,28},{8,16},{12,20},{16,8},{20,12},{24,0},{28,4},{1,25},{... | collective-permute-start | bytes 196616 | tf_op jit(solution)/shard_map/ppermute | solution.py:205
  52.7 12.5 %collective-permute-start.17 = (bf16[2,64,256]{2,1,0:T(8,128)(2,1)S(1)}, bf16[2,64,256]{2,1,0:T(8,128)(2,1)S(1)}, u32[]{:S(2)}, u32[]{:S(2)}) collective-permute-start(bf16[2,64,256]{2,1,0:T(8,128)(2,1)S(1)} %turn_leading.1), channel_id=1, source_target_pairs={{0,20},{4,16},{8,28},{12,24},{16,4},{20,0},{24,12},{28,8},{1,21},{... | collective-permute-start | bytes 196616 | tf_op jit(solution)/shard_map/ppermute | solution.py:205
  57.8 7.5 %collective-permute-start.18 = (bf16[2,64,256]{2,1,0:T(8,128)(2,1)S(1)}, bf16[2,64,256]{2,1,0:T(8,128)(2,1)S(1)}, u32[]{:S(2)}, u32[]{:S(2)}) collective-permute-start(bf16[2,64,256]{2,1,0:T(8,128)(2,1)S(1)} %turn_leading.1), channel_id=1, source_target_pairs={{0,16},{4,20},{8,24},{12,28},{16,0},{20,4},{24,8},{28,12},{1,17},{... | collective-permute-start | bytes 196616 | tf_op jit(solution)/shard_map/ppermute | solution.py:205
  58.3 7.0 %collective-permute-start.19 = (bf16[2,64,256]{2,1,0:T(8,128)(2,1)S(1)}, bf16[2,64,256]{2,1,0:T(8,128)(2,1)S(1)}, u32[]{:S(2)}, u32[]{:S(2)}) collective-permute-start(bf16[2,64,256]{2,1,0:T(8,128)(2,1)S(1)} %turn_leading.1), channel_id=1, source_target_pairs={{0,12},{4,8},{8,4},{12,0},{16,28},{20,24},{24,20},{28,16},{1,13},{... | collective-permute-start | bytes 196616 | tf_op jit(solution)/shard_map/ppermute | solution.py:205
  58.5 6.8 %collective-permute-start.20 = (bf16[2,64,256]{2,1,0:T(8,128)(2,1)S(1)}, bf16[2,64,256]{2,1,0:T(8,128)(2,1)S(1)}, u32[]{:S(2)}, u32[]{:S(2)}) collective-permute-start(bf16[2,64,256]{2,1,0:T(8,128)(2,1)S(1)} %turn_leading.1), channel_id=1, source_target_pairs={{0,8},{4,12},{8,0},{12,4},{16,24},{20,28},{24,16},{28,20},{1,9},{5... | collective-permute-start | bytes 196616 | tf_op jit(solution)/shard_map/ppermute | solution.py:205
  60.2 5.0 %collective-permute-start.21 = (bf16[2,64,256]{2,1,0:T(8,128)(2,1)S(1)}, bf16[2,64,256]{2,1,0:T(8,128)(2,1)S(1)}, u32[]{:S(2)}, u32[]{:S(2)}) collective-permute-start(bf16[2,64,256]{2,1,0:T(8,128)(2,1)S(1)} %turn_leading.1), channel_id=1, source_target_pairs={{0,4},{4,0},{8,12},{12,8},{16,20},{20,16},{24,28},{28,24},{1,5},{5... | collective-permute-start | bytes 196616 | tf_op jit(solution)/shard_map/ppermute | solution.py:205
  (8 other events, 6.5 us)

commit v2 on v0

v2 whole, which is shorter than its diff:
```python
import functools

import jax
import jax.numpy as jnp
from jax import lax
from jax.experimental import pallas as pl
from jax.experimental.pallas import tpu as pltpu
from jax.sharding import PartitionSpec as P

MOVE = 2
ITERS = 5
CORES = 2
PIECES = 4
VMEM_LIMIT = 14 * 1024 * 1024
LONG = 1 << 30

f32, bf16, i32 = jnp.float32, jnp.bfloat16, jnp.int32

SMEM = pl.BlockSpec(memory_space=pltpu.SMEM)
VMEM = pl.BlockSpec(memory_space=pltpu.VMEM)
HBM = pl.BlockSpec(memory_space=pltpu.HBM)
ANY = pl.BlockSpec(memory_space=pl.ANY)


def stay(x):
    return pltpu.with_memory_space_constraint(x, pltpu.HBM)


def call(kernel, name, outs, in_specs, out_specs, args, moved=1 << 20, scratch=(), aliases={}):
    return pl.pallas_call(
        kernel,
        out_shape=outs,
        in_specs=in_specs,
        out_specs=out_specs,
        scratch_shapes=scratch,
        input_output_aliases=aliases,
        compiler_params=pltpu.CompilerParams(vmem_limit_bytes=VMEM_LIMIT),
        cost_estimate=pl.CostEstimate(flops=16 * moved if moved == LONG else 0, bytes_accessed=moved, transcendentals=0),
        name=name,
    )(*args)


def assign_slots(bl, ln, first_rows, slot_of_list, plan, crossing):
    blocks, lists = bl.shape[0], slot_of_list.shape[0]
    for l in range(lists):
        slot_of_list[l] = -1

    def visit(b, nxt, wanted):
        l = bl[b]
        s = slot_of_list[l]
        new = jnp.logical_and(s < 0, wanted)
        slot_of_list[l] = jnp.where(new, nxt, s)
        return nxt + new.astype(i32)

    nxt = jnp.int32(0)
    for b in range(MOVE):
        nxt = visit(b, nxt, True)
    for b in range(MOVE, blocks):
        nxt = visit(b, nxt, ln[b] > first_rows)
    crossing[0] = nxt
    for b in range(MOVE, blocks):
        nxt = visit(b, nxt, True)
    plan[blocks] = nxt
    for b in range(blocks):
        plan[b] = slot_of_list[bl[b]]


def gram_kernel(bounds, bl_hbm, ln_hbm, points_hbm, targets_hbm, centroids_hbm, plan, crossing, residual, *refs):
    n = len(bounds)
    keeps = refs[:n]
    sends = refs[n:n + 2]
    bl, ln, slot_of_list, points, targets, centroids, acc, sems, int_sems = refs[n + 2:]
    blocks, rows, _ = points.shape
    piece = blocks // PIECES
    copies = [
        pltpu.make_async_copy(bl_hbm, bl, int_sems.at[0]),
        pltpu.make_async_copy(ln_hbm, ln, int_sems.at[1]),
        pltpu.make_async_copy(centroids_hbm, centroids, int_sems.at[2]),
    ]
    for copy in copies:
        copy.start()
    parts = []
    for i in range(PIECES):
        at = pl.ds(i * piece, piece)
        pair = (
            pltpu.make_async_copy(points_hbm.at[at], points.at[at], sems.at[0, i]),
            pltpu.make_async_copy(targets_hbm.at[at], targets.at[at], sems.at[1, i]),
        )
        for copy in pair:
            copy.start()
        parts.append(pair)
    me = lax.axis_index("narrow")
    core = lax.rem(me, CORES)
    copies[0].wait()
    copies[1].wait()
    assign_slots(bl, ln, CORES * rows, slot_of_list, plan, crossing)
    acc[...] = jnp.zeros_like(acc)
    copies[2].wait()
    row_ids = lax.broadcasted_iota(i32, points.shape[1:], 0) + me * rows
    for i in range(PIECES):
        for copy in parts[i]:
            copy.wait()

        @pl.loop(i * piece, (i + 1) * piece, unroll=4)
        def _(b):
            slot = plan[b]
            kept = row_ids < ln[b]
            res = jnp.where(kept, points[b].astype(f32) - centroids[pl.ds(bl[b], 1), :], 0.0).astype(bf16)
            residual[b] = res
            acc[slot] += lax.dot_general(res, targets[b], (((0,), (0,)), ((), ())), preferred_element_type=f32)

    for (s, count), keep in zip(bounds, keeps):
        for i in range(count):
            at = CORES * (s + i)
            keep[i] = acc[at + core]
            send, j = (sends[0], i) if s == 0 else (sends[1], s + i - bounds[0][1])
            send[j] = acc[at + 1 - core].astype(bf16)


def sum_kernel(bounds, base, *refs):
    n = len(bounds)
    keeps, recv, sums = refs[:n], refs[n], refs[-n:]
    for (s, count), keep, out in zip(bounds, keeps, sums):
        at = s - base
        out[...] = (keep[...] + recv[at:at + count].astype(f32)).astype(bf16)


def newton_kernel(count, extra, first, offset, keep, recv, *refs):
    extras, out = refs[:extra], refs[-1]

    def run():
        xs = []
        for i in range(count):
            g = keep[i] + recv[offset + i].astype(f32)
            for e in extras:
                g = g + e[i].astype(f32)
            xs.append(g * lax.rsqrt(jnp.sum(g * g) + 1e-6))
        for _ in range(ITERS):
            for i in range(count):
                x = xs[i]
                xb = x.astype(bf16)
                p = lax.dot_general(xb, xb, (((1,), (1,)), ((), ())), preferred_element_type=f32).astype(bf16)
                xs[i] = 1.5 * x - 0.5 * jnp.dot(p, xb, preferred_element_type=f32)
        for i in range(count):
            out[i] = xs[i].astype(bf16)

    if first is None:
        run()
    else:
        plan = refs[-2]
        used = plan[plan.shape[0] - 1] > CORES * first
        pl.when(used)(run)

        @pl.when(jnp.logical_not(used))
        def _():
            out[...] = jnp.zeros_like(out)


def newton(keep, recv, extras, after, first, offset, plan=None, moved=1 << 20):
    count, width = keep.shape[:2]
    args = (keep, recv) + tuple(extras) + tuple(after)
    specs = [VMEM] * (2 + len(extras)) + [ANY] * len(after)
    if plan is not None:
        args, specs = args + (plan,), specs + [SMEM]
    return call(
        functools.partial(newton_kernel, count, len(extras), first if plan is not None else None, offset),
        "newton",
        jax.ShapeDtypeStruct(keep.shape, bf16),
        specs,
        VMEM,
        args,
        moved=moved,
    )


def leading_kernel(plan, residual, own, sibling, out):
    core = lax.rem(lax.axis_index("narrow"), CORES)
    for b in range(MOVE):
        mine = lax.rem(plan[b], CORES) == core
        rotation = jnp.where(mine, own[0], sibling[0])
        out[b] = jnp.dot(residual[b], rotation, preferred_element_type=f32).astype(bf16)


def pair_kernel(near, far, _, out):
    out[0] = near[...]
    out[1] = far[...]


def turn_kernel(starts, hops, plan, sources, residual, *refs):
    n = len(starts)
    owns, siblings = refs[:n], refs[n:2 * n]
    parts = refs[2 * n:2 * n + len(hops)]
    out, rots, turned, sems = refs[2 * n + len(hops):]
    blocks, rows, _ = residual.shape
    piece = blocks // PIECES
    core = lax.rem(lax.axis_index("narrow"), CORES)
    here = lax.axis_index("wide")
    for s, o, t in zip(starts, owns, siblings):
        for i in range(o.shape[0]):
            rots[CORES * (s + i) + core] = o[i]
            rots[CORES * (s + i) + 1 - core] = t[i]
    for j in range(MOVE):
        donor = sources[j] // blocks
        picked = parts[0][0, j]
        for part, group in zip(parts, hops):
            for i, hop in enumerate(group):
                match = donor == (hop if len(parts) == 1 else here ^ hop)
                picked = jnp.where(match, part[i, j], picked)
        turned[j] = picked
    copies = []
    for i in range(PIECES):
        @pl.loop(max(MOVE, i * piece), (i + 1) * piece, unroll=True)
        def _(b):
            turned[b] = jnp.dot(residual[b], rots[plan[b]], preferred_element_type=f32).astype(bf16)

        at = pl.ds(i * piece, piece)
        copies.append(pltpu.make_async_copy(turned.at[at], out.at[at], sems.at[i]))
        copies[-1].start()
    for copy in copies:
        copy.wait()


def turn_rest_kernel(first, plan, residual, own, sibling, _, out, block):
    core = lax.rem(lax.axis_index("narrow"), CORES)

    @pl.loop(MOVE, residual.shape[0])
    def _(b):
        @pl.when(plan[b] >= first)
        def _():
            at = lax.div(plan[b] - first, CORES)
            mine = lax.rem(plan[b], CORES) == core
            rotation = jnp.where(mine, own[at], sibling[at])
            block[...] = jnp.dot(residual[b], rotation, preferred_element_type=f32).astype(bf16)
            pltpu.sync_copy(block, out.at[b])


def chunk_bounds(per, capped):
    cap = per * 3 // 4 if capped else per
    sizes, left = [1], cap - 1
    while left > 1:
        sizes.append(min(2, left - 1))
        left -= sizes[-1]
    if left:
        sizes.append(left)
    bounds = [(sum(sizes[:i]), size) for i, size in enumerate(sizes)]
    return bounds, [(cap, per - cap)] if cap < per else []


def local(wide, narrow, points, targets, centroids, block_list, lengths, sources):
    blocks, rows, width = points.shape
    lists = centroids.shape[0]
    per = lists // CORES
    chips = narrow // CORES
    mat = (width, width)
    bounds, rest = chunk_bounds(per, chips == 2)
    all_bounds = bounds + rest

    n = len(all_bounds)
    lead = all_bounds[0][1]
    grams = call(
        functools.partial(gram_kernel, all_bounds),
        "grams",
        (jax.ShapeDtypeStruct((blocks + 1,), i32), jax.ShapeDtypeStruct((1,), i32), jax.ShapeDtypeStruct(points.shape, bf16))
        + tuple(jax.ShapeDtypeStruct((count,) + mat, f32) for _, count in all_bounds)
        + tuple(jax.ShapeDtypeStruct((count,) + mat, bf16) for count in (lead, per - lead)),
        [HBM] * 5,
        (SMEM, SMEM) + (VMEM,) * (3 + n),
        tuple(stay(x) for x in (block_list, lengths, points, targets, centroids)),
        scratch=[
            pltpu.SMEM((blocks,), i32),
            pltpu.SMEM((blocks,), i32),
            pltpu.SMEM((lists,), i32),
            pltpu.VMEM(points.shape, bf16),
            pltpu.VMEM(points.shape, bf16),
            pltpu.VMEM(centroids.shape, f32),
            pltpu.VMEM((lists,) + mat, f32),
            pltpu.SemaphoreType.DMA((2, PIECES)),
            pltpu.SemaphoreType.DMA((3,)),
        ],
    )
    plan, crossing, residual = grams[:3]
    keeps, sends = grams[3:3 + n], grams[3 + n:]

    to_core = [(i, i ^ 1) for i in range(narrow)]
    to_chip = [[(i, (i + CORES * k) % narrow) for i in range(narrow)] for k in range(1, chips)]

    def cross(part):
        return tuple(lax.ppermute(part, "narrow", perm) for perm in to_chip)

    def sums_of(some, recv, base, after=(), keeps=keeps):
        return call(
            functools.partial(sum_kernel, all_bounds[some], base),
            "chip_sums",
            tuple(jax.ShapeDtypeStruct((count,) + mat, bf16) for _, count in all_bounds[some]),
            [VMEM] * (1 + len(all_bounds[some])) + [ANY] * len(after),
            (VMEM,) * len(all_bounds[some]),
            (*(keeps[some] if len(keeps) == n else keeps), recv, *after),
        )

    recvs = [lax.ppermute(send, "narrow", to_core) for send in sends]
    sums = sums_of(slice(0, 1), recvs[0], 0)
    m = len(bounds)
    sums += sums_of(slice(1, m), recvs[1], lead, sums)
    crossed = [cross(part) for part in sums[:len(bounds)]]
    crossed += [()] * len(rest)

    owns, siblings = [None] * n, [None] * n

    def polar(i, after=(), gate=None):
        s = all_bounds[i][0]
        recv, offset = (recvs[0], 0) if i == 0 else (recvs[1], s - lead)
        owns[i] = newton(keeps[i], recv, crossed[i], after, s, offset, gate, LONG if 2 <= i < len(bounds) else 1 << 20)
        siblings[i] = lax.ppermute(owns[i], "narrow", to_core)

    if rest:
        polar(n - 1, sums, plan)
    polar(0, (owns[-1],) if rest else ())

    leading = call(
        leading_kernel,
        "turn_leading",
        jax.ShapeDtypeStruct((MOVE, rows, width), bf16),
        [SMEM] + [VMEM] * 3,
        VMEM,
        (plan, residual, owns[0], siblings[0]),
    )
    if wide <= 16 and wide & (wide - 1) == 0:
        half = wide // 2
        far = lax.ppermute(leading, "wide", [(i, i ^ half) for i in range(wide)])
        polar(1, (leading,))
        pair = call(
            pair_kernel,
            "pair",
            jax.ShapeDtypeStruct((2,) + leading.shape, bf16),
            [VMEM, VMEM, ANY],
            VMEM,
            (leading, far, owns[1]),
        )
        parts = [pair] + [lax.ppermute(pair, "wide", [(i, i ^ k) for i in range(wide)]) for k in range(1, half)]
        hops = [(k, k ^ half) for k in range(half)]
    else:
        polar(1, (leading,))
        parts = [lax.all_gather(leading, "wide", axis=0)]
        hops = [tuple(range(wide))]

    for i in range(2, len(bounds)):
        polar(i, (owns[i - 1],) if i > 2 else (owns[1], parts[0]))

    turned = call(
        functools.partial(turn_kernel, [s for s, _ in all_bounds], hops),
        "turn",
        pltpu.HBM(points.shape, bf16),
        [SMEM] * 2 + [VMEM] * (1 + 2 * n + len(parts)),
        HBM,
        (plan, sources, residual, *owns, *siblings, *parts),
        scratch=[
            pltpu.VMEM((lists,) + mat, bf16),
            pltpu.VMEM(points.shape, bf16),
            pltpu.SemaphoreType.DMA((PIECES,)),
        ],
    )
    if not rest:
        return turned

    def exchange_rest(_, state):
        turned, keep = state
        chip = sums_of(slice(m, n), recvs[1], lead, keeps=(keep,))[0]
        own = newton(keep, recvs[1], cross(chip), (), None, rest[0][0] - lead)
        sibling = lax.ppermute(own, "narrow", to_core)
        turned = call(
            functools.partial(turn_rest_kernel, CORES * rest[0][0]),
            "turn_rest",
            pltpu.HBM(turned.shape, bf16),
            [SMEM] + [VMEM] * 3 + [HBM],
            HBM,
            (plan, residual, own, sibling, stay(turned)),
            scratch=[pltpu.VMEM((rows, width), bf16)],
            aliases={4: 0},
        )
        return turned, own.astype(f32)

    overflow = (crossing[0] > CORES * rest[0][0]).astype(i32)
    return lax.fori_loop(0, overflow, exchange_rest, (turned, keeps[-1]))[0]


def solution(mesh):
    return jax.shard_map(
        functools.partial(local, mesh.shape["wide"], mesh.shape["narrow"]),
        mesh=mesh,
        in_specs=(
            P("wide", "narrow", None),
            P("wide", "narrow", None),
            P("wide", None),
            P("wide"),
            P("wide"),
            P("wide"),
        ),
        out_specs=P("wide", "narrow", None),
        check_vma=False,
    )
```

time: 159 us -> 44.4 us (0.28)
  waiting for transfers between devices: 69.8 us -> 11.4 us
  matrix products: 36.3 us -> 0 us
  blocking collectives: 31.5 us -> 0 us
  Pallas kernels: 0 us -> 17.3 us
  starting transfers between devices: 0.22 us -> 14.7 us
  between operations: 13.6 us -> 0.77 us
  local copies, waits for them, and re-layouts: 4.46 us -> 0.01 us
  other arithmetic: 3.3 us -> 0 us
    reduce_scatter x1 -> x0, waiting for transfers between devices: 47.1 us -> none  [local(): lax.psum_scatter(jnp.einsum('bl,bde->lde', list_pick, block_grams, precis...]
    dot_general x16 -> x0, matrix products: 36.3 us -> none  [the longest x1 8.11 us: local(): jnp.einsum('bl,bde->lde', list_pick, block_grams, precision=highest_prec)]
    all_gather x1 -> x0, blocking collectives: 31.5 us -> none  [local(): part_rows = lax.all_gather(turned[None, :MOVE], 'wide', axis=0, tiled=True)]
    all_gather x1 -> x0, waiting for transfers between devices: 22.6 us -> none  [local(): all_rotations = lax.all_gather(rotation, 'narrow', axis=0, tiled=True)]
    pallas_call x0 -> x11, Pallas kernels: none -> 17.3 us  [call(): pl.pallas_call(kernel, out_shape=outs, in_specs=in_specs, out_specs=out_s...]
    ppermute x0 -> x15, starting transfers between devices: none -> 14.7 us  [the longest x4 6.48 us: cross(): return tuple((lax.ppermute(part, 'narrow', perm) for perm in to_chip))]
    ppermute x0 -> x15, waiting for transfers between devices: none -> 11.4 us  [the longest x3 5.72 us: local(): lax.ppermute(pair, 'wide', [(i, i ^ k) for i in range(wide)])]
    dot_general x2 -> x0, local copies, waits for them, and re-layouts: 4.37 us -> none  [the longest x1 4.36 us: local(): jnp.einsum('bl,bde->lde', list_pick, block_grams, precision=highest_prec)]
  transfers between devices with their start and end apart: 2 -> 15, of which waited for: 2 -> 9; matrix products, arithmetic and copies ran while one was open for 0% -> 0% of each run, Pallas kernels for 0% -> 21%
where the time goes in v2:
time: 44.4 us; the launch traced here: 44.2 us
  Pallas kernels  17.3 us (39%)
  starting transfers between devices  14.7 us (33%)
  waiting for transfers between devices  11.4 us (26%)
  between operations  0.77 us (2%)
    pallas_call x11, Pallas kernels, call(): pl.pallas_call(kernel, out_shape=outs, in_specs=in_specs, out_specs=out_s...  17.3 us
    ppermute x4, starting transfers between devices, cross(): return tuple((lax.ppermute(part, 'narrow', perm) for perm in to_chip))  6.48 us
    ppermute x3, waiting for transfers between devices, local(): lax.ppermute(pair, 'wide', [(i, i ^ k) for i in range(wide)])  5.72 us
    ppermute x3, starting transfers between devices, local(): lax.ppermute(pair, 'wide', [(i, i ^ k) for i in range(wide)])  3.64 us
    ppermute x1, starting transfers between devices, local(): far = lax.ppermute(leading, 'wide', [(i, i ^ half) for i in range(wide)])  3.25 us
    ppermute x2, waiting for transfers between devices, local(): recvs = [lax.ppermute(send, 'narrow', to_core) for send in sends]  2.21 us
    ppermute x4, waiting for transfers between devices, cross(): return tuple((lax.ppermute(part, 'narrow', perm) for perm in to_chip))  1.9 us
    ppermute x5, waiting for transfers between devices, polar(): siblings[i] = lax.ppermute(owns[i], 'narrow', to_core)  1.35 us
  transfers between devices with their start and end apart: 15, of which 9 were waited for; matrix products, arithmetic and copies ran while one was open for 0% of the time, Pallas kernels for 21%

profile of v2, /device:TPU:0, one launch (start us, length us, event | category | flops | bytes accessed | tf_op | source)
XLA Modules:
  0.0 44.2 jit_solution(6507182433797649504)
XLA Ops:
  0.0 5.0 %grams.1 = (s32[33]{0:T(128)S(1)}, s32[1]{0:T(128)}, bf16[32,64,256]{2,1,0:T(8,128)(2,1)S(1)}, f32[1,256,256]{2,1,0:T(8,128)S(1)}, f32[2,256,256]{2,1,0:T(8,128)...) custom-call(s32[32]{0:T(128)} %bl_hbm.1, ...), custom_call_target="tpu_custom_call" | custom-call | bytes 1048576 | tf_op jit(solution)/shard_map/grams/pallas_call | solution.py:30
  5.1 0.5 %collective-permute-start.4 = (bf16[7,256,256]{2,1,0:T(8,128)(2,1)S(1)}, bf16[7,256,256]{2,1,0:T(8,128)(2,1)S(1)}, u32[]{:S(2)}, u32[]{:S(2)}) collective-permute-start(bf16[7,256,256]{2,1,0:T(8,128)(2,1)S(1)} %get-tuple-element.61), channel_id=1, source_target_pairs={{0,1},{1,0},{2,3},{3,2},{4,5},{5,4},{6,7},{7,6},{8,9},{9,8},{10,11... | collective-permute-start | bytes 2752520 | tf_op jit(solution)/shard_map/ppermute | solution.py:300
  5.7 2.2 %collective-permute-done.2.refs_1_.recv = bf16[1,256,256]{2,1,0:T(8,128)(2,1)S(1)} collective-permute-done((bf16[1,256,256]{2,1,0:T(8,128)(2,1)S(1)}, bf16[1,256,256]{2,1,0:T(8,128)(2,1)S(1)}, u32[]{:S(2)}, u32[]{:S(2)}) %collective-permute-start.2) | collective-permute-done | bytes 131104 | tf_op jit(solution)/shard_map/ppermute | solution.py:300
  7.9 2.9 %collective-permute-start.3 = (bf16[1,256,256]{2,1,0:T(8,128)(2,1)S(1)}, bf16[1,256,256]{2,1,0:T(8,128)(2,1)S(1)}, u32[]{:S(2)}, u32[]{:S(2)}) collective-permute-start(bf16[1,256,256]{2,1,0:T(8,128)(2,1)S(1)} %chip_sums.3.refs_4_.refs_0_), channel_id=1, source_target_pairs={{0,2},{1,3},{2,0},{3,1},{4,6},{5,7},{6,4},{7,5},{8,10},{9,11},{10,... | collective-permute-start | bytes 393224 | tf_op jit(solution)/shard_map/ppermute | solution.py:288
  11.0 2.0 %collective-permute-start.7 = (bf16[2,256,256]{2,1,0:T(8,128)(2,1)S(1)}, bf16[2,256,256]{2,1,0:T(8,128)(2,1)S(1)}, u32[]{:S(2)}, u32[]{:S(2)}) collective-permute-start(bf16[2,256,256]{2,1,0:T(8,128)(2,1)S(1)} %get-tuple-element.66.refs_2_), channel_id=1, source_target_pairs={{0,2},{1,3},{2,0},{3,1},{4,6},{5,7},{6,4},{7,5},{8,10},{9,11},{10,... | collective-permute-start | bytes 786440 | tf_op jit(solution)/shard_map/ppermute | solution.py:288
  13.0 0.6 %newton.6.refs_1_.refs_4_ = bf16[2,256,256]{2,1,0:T(8,128)(2,1)S(1)} custom-call(f32[2,256,256]{2,1,0:T(8,128)S(1)} %get-tuple-element.130.keep, bf16[7,256,256]{2,1,0:T(8,128)(2,1)S(1)} %collective-permute-done.4.refs_3_.recv, bf16[1,256,256]{2,1,0:T(8,128)(2,1)S(1)} %chip_sums.3.refs_4_.refs_0_, bf16[2,256,256]{2,1,0:T(8,128)(2,1)S(1)} %get-tuple-element.65.refs_1_, ...), custom_call_target="tpu_custom_call" | custom-call | bytes 1048576 | tf_op jit(solution)/shard_map/newton/pallas_call | solution.py:30
  13.6 1.5 %collective-permute-done.3.refs_0_ = bf16[1,256,256]{2,1,0:T(8,128)(2,1)S(1)} collective-permute-done((bf16[1,256,256]{2,1,0:T(8,128)(2,1)S(1)}, bf16[1,256,256]{2,1,0:T(8,128)(2,1)S(1)}, u32[]{:S(2)}, u32[]{:S(2)}) %collective-permute-start.3) | collective-permute-done | bytes 131104 | tf_op jit(solution)/shard_map/ppermute | solution.py:288
  15.1 1.8 %newton.7.own.refs_0_ = bf16[1,256,256]{2,1,0:T(8,128)(2,1)S(1)} custom-call(f32[1,256,256]{2,1,0:T(8,128)S(1)} %get-tuple-element.58.refs_0_.keep, bf16[1,256,256]{2,1,0:T(8,128)(2,1)S(1)} %collective-permute-done.2.refs_1_.recv, bf16[1,256,256]{2,1,0:T(8,128)(2,1)S(1)} %collective-permute-done.3.refs_0_, bf16[2,256,256]{2,1,0:T(8,128)(2,1)S(1)} %newton.6.refs_1_.refs_4_), custom_call_target="tpu_custom_call" | custom-call | bytes 1048576 | tf_op jit(solution)/shard_map/newton/pallas_call | solution.py:30
  17.0 1.3 %collective-permute-done.6.sibling.refs_5_ = bf16[1,256,256]{2,1,0:T(8,128)(2,1)S(1)} collective-permute-done((bf16[1,256,256]{2,1,0:T(8,128)(2,1)S(1)}, bf16[1,256,256]{2,1,0:T(8,128)(2,1)S(1)}, u32[]{:S(2)}, u32[]{:S(2)}) %collective-permute-start.6) | collective-permute-done | bytes 131104 | tf_op jit(solution)/shard_map/ppermute | solution.py:313
  18.4 0.7 %turn_leading.1.refs_1_.near = bf16[2,64,256]{2,1,0:T(8,128)(2,1)S(1)} custom-call(s32[33]{0:T(128)S(1)} %get-tuple-element.133.refs_4_.plan, bf16[32,64,256]{2,1,0:T(8,128)(2,1)S(1)} %get-tuple-element.134.residual, bf16[1,256,256]{2,1,0:T(8,128)(2,1)S(1)} %newton.7.own.refs_0_, bf16[1,256,256]{2,1,0:T(8,128)(2,1)S(1)} %collective-permute-done.6.sibling.refs_5_), custom_call_target="tpu_custom_call" | custom-call | bytes 1048576 | tf_op jit(solution)/shard_map/turn_leading/pallas_call | solution.py:30
  19.1 3.2 %collective-permute-start.8 = (bf16[2,64,256]{2,1,0:T(8,128)(2,1)S(1)}, bf16[2,64,256]{2,1,0:T(8,128)(2,1)S(1)}, u32[]{:S(2)}, u32[]{:S(2)}) collective-permute-start(bf16[2,64,256]{2,1,0:T(8,128)(2,1)S(1)} %turn_leading.1.refs_1_.near), channel_id=1, source_target_pairs={{0,16},{4,20},{8,24},{12,28},{16,0},{20,4},{24,8},{28,12},{1,17},{... | collective-permute-start | bytes 196616 | tf_op jit(solution)/shard_map/ppermute | solution.py:329
  22.3 1.5 %collective-permute-start.9 = (bf16[1,256,256]{2,1,0:T(8,128)(2,1)S(1)}, bf16[1,256,256]{2,1,0:T(8,128)(2,1)S(1)}, u32[]{:S(2)}, u32[]{:S(2)}) collective-permute-start(bf16[1,256,256]{2,1,0:T(8,128)(2,1)S(1)} %get-tuple-element.67.refs_3_), channel_id=1, source_target_pairs={{0,2},{1,3},{2,0},{3,1},{4,6},{5,7},{6,4},{7,5},{8,10},{9,11},{10,... | collective-permute-start | bytes 393224 | tf_op jit(solution)/shard_map/ppermute | solution.py:288
  23.8 2.1 %newton.8._.refs_1_ = bf16[2,256,256]{2,1,0:T(8,128)(2,1)S(1)} custom-call(f32[2,256,256]{2,1,0:T(8,128)S(1)} %get-tuple-element.62.refs_0_.keep, bf16[7,256,256]{2,1,0:T(8,128)(2,1)S(1)} %collective-permute-done.4.refs_3_.recv, bf16[2,256,256]{2,1,0:T(8,128)(2,1)S(1)} %collective-permute-done.5.refs_0_, bf16[2,64,256]{2,1,0:T(8,128)(2,1)S(1)} %turn_leading.1.refs_1_.near), custom_call_target="tpu_custom_call" | custom-call | bytes 1048576 | tf_op jit(solution)/shard_map/newton/pallas_call | solution.py:30
  25.9 0.2 collective-permute-done.8.far
  26.3 2.1 %newton.9.refs_1_.refs_2_ = bf16[2,256,256]{2,1,0:T(8,128)(2,1)S(1)} custom-call(f32[2,256,256]{2,1,0:T(8,128)S(1)} %get-tuple-element.63.refs_1_.keep, bf16[7,256,256]{2,1,0:T(8,128)(2,1)S(1)} %collective-permute-done.4.refs_3_.recv, bf16[2,256,256]{2,1,0:T(8,128)(2,1)S(1)} %collective-permute-done.7.refs_0_, bf16[2,256,256]{2,1,0:T(8,128)(2,1)S(1)} %newton.8._.refs_1_, ...), custom_call_target="tpu_custom_call" | custom-call | flops 17179869184 | bytes 1073741824 | tf_op jit(solution)/shard_map/newton/pallas_call | solution.py:30
  28.4 0.2 collective-permute-done.9.refs_0_
  28.7 1.8 %newton.10.refs_3_ = bf16[1,256,256]{2,1,0:T(8,128)(2,1)S(1)} custom-call(f32[1,256,256]{2,1,0:T(8,128)S(1)} %get-tuple-element.64.refs_2_.keep, bf16[7,256,256]{2,1,0:T(8,128)(2,1)S(1)} %collective-permute-done.4.refs_3_.recv, bf16[1,256,256]{2,1,0:T(8,128)(2,1)S(1)} %collective-permute-done.9.refs_0_, bf16[2,256,256]{2,1,0:T(8,128)(2,1)S(1)} %newton.9.refs_1_.refs_2_), custom_call_target="tpu_custom_call" | custom-call | flops 17179869184 | bytes 1073741824 | tf_op jit(solution)/shard_map/newton/pallas_call | solution.py:30
  30.6 0.5 %collective-permute-start.11 = (bf16[2,256,256]{2,1,0:T(8,128)(2,1)S(1)}, bf16[2,256,256]{2,1,0:T(8,128)(2,1)S(1)}, u32[]{:S(2)}, u32[]{:S(2)}) collective-permute-start(bf16[2,256,256]{2,1,0:T(8,128)(2,1)S(1)} %newton.9.refs_1_.refs_2_), channel_id=1, source_target_pairs={{0,1},{1,0},{2,3},{3,2},{4,5},{5,4},{6,7},{7,6},{8,9},{9,8},{10,11... | collective-permute-start | bytes 786440 | tf_op jit(solution)/shard_map/ppermute | solution.py:313
  31.2 1.9 %collective-permute-start.14 = (bf16[2,2,64,256]{3,2,1,0:T(8,128)(2,1)S(1)}, bf16[2,2,64,256]{3,2,1,0:T(8,128)(2,1)S(1)}, u32[]{:S(2)}, u32[]{:S(2)}) collective-permute-start(bf16[2,2,64,256]{3,2,1,0:T(8,128)(2,1)S(1)} %pair.1.refs_2_.refs_10_), channel_id=1, source_target_pairs={{0,4},{4,0},{8,12},{12,8},{16,20},{20,16},{24,28},{28,24},{1,5},{5... | collective-permute-start | bytes 393224 | tf_op jit(solution)/shard_map/ppermute | solution.py:339
  33.0 1.6 %collective-permute-start.15 = (bf16[2,2,64,256]{3,2,1,0:T(8,128)(2,1)S(1)}, bf16[2,2,64,256]{3,2,1,0:T(8,128)(2,1)S(1)}, u32[]{:S(2)}, u32[]{:S(2)}) collective-permute-start(bf16[2,2,64,256]{3,2,1,0:T(8,128)(2,1)S(1)} %pair.1.refs_2_.refs_10_), channel_id=1, source_target_pairs={{0,8},{4,12},{8,0},{12,4},{16,24},{20,28},{24,16},{28,20},{1,9},{5... | collective-permute-start | bytes 393224 | tf_op jit(solution)/shard_map/ppermute | solution.py:339
  35.5 1.7 %collective-permute-done.14.refs_11_ = bf16[2,2,64,256]{3,2,1,0:T(8,128)(2,1)S(1)} collective-permute-done((bf16[2,2,64,256]{3,2,1,0:T(8,128)(2,1)S(1)}, bf16[2,2,64,256]{3,2,1,0:T(8,128)(2,1)S(1)}, u32[]{:S(2)}, u32[]{:S(2)}) %collective-permute-start.14) | collective-permute-done | bytes 131104 | tf_op jit(solution)/shard_map/ppermute | solution.py:339
  37.1 2.3 %collective-permute-done.15.refs_12_ = bf16[2,2,64,256]{3,2,1,0:T(8,128)(2,1)S(1)} collective-permute-done((bf16[2,2,64,256]{3,2,1,0:T(8,128)(2,1)S(1)}, bf16[2,2,64,256]{3,2,1,0:T(8,128)(2,1)S(1)}, u32[]{:S(2)}, u32[]{:S(2)}) %collective-permute-start.15) | collective-permute-done | bytes 131104 | tf_op jit(solution)/shard_map/ppermute | solution.py:339
  39.4 1.8 %collective-permute-done.16.refs_13_ = bf16[2,2,64,256]{3,2,1,0:T(8,128)(2,1)S(1)} collective-permute-done((bf16[2,2,64,256]{3,2,1,0:T(8,128)(2,1)S(1)}, bf16[2,2,64,256]{3,2,1,0:T(8,128)(2,1)S(1)}, u32[]{:S(2)}, u32[]{:S(2)}) %collective-permute-start.16) | collective-permute-done | bytes 131104 | tf_op jit(solution)/shard_map/ppermute | solution.py:339
  41.2 3.0 %turn.1 = bf16[32,64,256]{2,1,0:T(8,128)(2,1)} custom-call(s32[33]{0:T(128)S(1)} %get-tuple-element.133.refs_4_.plan, s32[32]{0:T(128)S(1)} %copy-done, bf16[32,64,256]{2,1,0:T(8,128)(2,1)} %copy-done.3, bf16[1,256,256]{2,1,0:T(8,128)(2,1)S(1)} %newton.7.own.refs_0_, bf16[2,256,256]{2,1,0:T(8,128)(2,1)S(1)} %newton.8._.refs_1_, ...), custom_call_target="tpu_custom_call" | custom-call | bytes 1048576 | tf_op jit(solution)/shard_map/turn/pallas_call | solution.py:30
  (24 shorter events, 0.9 us)
Async XLA Ops:
  5.0 8.0 %copy-start.1 = (f32[2,256,256]{2,1,0:T(8,128)}, f32[2,256,256]{2,1,0:T(8,128)S(1)}, u32[]{:S(2)}) copy-start(f32[2,256,256]{2,1,0:T(8,128)S(1)} %get-tuple-element.130.keep) | copy-start | bytes 1572868
  5.0 13.3 %copy-start.3 = (bf16[32,64,256]{2,1,0:T(8,128)(2,1)}, bf16[32,64,256]{2,1,0:T(8,128)(2,1)S(1)}, u32[]{:S(2)}) copy-start(bf16[32,64,256]{2,1,0:T(8,128)(2,1)S(1)} %get-tuple-element.134.residual) | copy-start | bytes 3145732
  5.1 5.8 %collective-permute-start.4 = (bf16[7,256,256]{2,1,0:T(8,128)(2,1)S(1)}, bf16[7,256,256]{2,1,0:T(8,128)(2,1)S(1)}, u32[]{:S(2)}, u32[]{:S(2)}) collective-permute-start(bf16[7,256,256]{2,1,0:T(8,128)(2,1)S(1)} %get-tuple-element.61), channel_id=1, source_target_pairs={{0,1},{1,0},{2,3},{3,2},{4,5},{5,4},{6,7},{7,6},{8,9},{9,8},{10,11... | collective-permute-start | bytes 2752520 | tf_op jit(solution)/shard_map/ppermute | solution.py:300
  5.6 2.3 %collective-permute-start.2 = (bf16[1,256,256]{2,1,0:T(8,128)(2,1)S(1)}, bf16[1,256,256]{2,1,0:T(8,128)(2,1)S(1)}, u32[]{:S(2)}, u32[]{:S(2)}) collective-permute-start(bf16[1,256,256]{2,1,0:T(8,128)(2,1)S(1)} %get-tuple-element.59), channel_id=1, source_target_pairs={{0,1},{1,0},{2,3},{3,2},{4,5},{5,4},{6,7},{7,6},{8,9},{9,8},{10,11... | collective-permute-start | bytes 393224 | tf_op jit(solution)/shard_map/ppermute | solution.py:300
  7.9 7.2 %collective-permute-start.3 = (bf16[1,256,256]{2,1,0:T(8,128)(2,1)S(1)}, bf16[1,256,256]{2,1,0:T(8,128)(2,1)S(1)}, u32[]{:S(2)}, u32[]{:S(2)}) collective-permute-start(bf16[1,256,256]{2,1,0:T(8,128)(2,1)S(1)} %chip_sums.3.refs_4_.refs_0_), channel_id=1, source_target_pairs={{0,2},{1,3},{2,0},{3,1},{4,6},{5,7},{6,4},{7,5},{8,10},{9,11},{10,... | collective-permute-start | bytes 393224 | tf_op jit(solution)/shard_map/ppermute | solution.py:288
  10.9 12.9 %collective-permute-start.5 = (bf16[2,256,256]{2,1,0:T(8,128)(2,1)S(1)}, bf16[2,256,256]{2,1,0:T(8,128)(2,1)S(1)}, u32[]{:S(2)}, u32[]{:S(2)}) collective-permute-start(bf16[2,256,256]{2,1,0:T(8,128)(2,1)S(1)} %get-tuple-element.65.refs_1_), channel_id=1, source_target_pairs={{0,2},{1,3},{2,0},{3,1},{4,6},{5,7},{6,4},{7,5},{8,10},{9,11},{10,... | collective-permute-start | bytes 786440 | tf_op jit(solution)/shard_map/ppermute | solution.py:288
  11.0 15.3 %collective-permute-start.7 = (bf16[2,256,256]{2,1,0:T(8,128)(2,1)S(1)}, bf16[2,256,256]{2,1,0:T(8,128)(2,1)S(1)}, u32[]{:S(2)}, u32[]{:S(2)}) collective-permute-start(bf16[2,256,256]{2,1,0:T(8,128)(2,1)S(1)} %get-tuple-element.66.refs_2_), channel_id=1, source_target_pairs={{0,2},{1,3},{2,0},{3,1},{4,6},{5,7},{6,4},{7,5},{8,10},{9,11},{10,... | collective-permute-start | bytes 786440 | tf_op jit(solution)/shard_map/ppermute | solution.py:288
  16.9 1.4 %collective-permute-start.6 = (bf16[1,256,256]{2,1,0:T(8,128)(2,1)S(1)}, bf16[1,256,256]{2,1,0:T(8,128)(2,1)S(1)}, u32[]{:S(2)}, u32[]{:S(2)}) collective-permute-start(bf16[1,256,256]{2,1,0:T(8,128)(2,1)S(1)} %newton.7.own.refs_0_), channel_id=1, source_target_pairs={{0,1},{1,0},{2,3},{3,2},{4,5},{5,4},{6,7},{7,6},{8,9},{9,8},{10,11... | collective-permute-start | bytes 393224 | tf_op jit(solution)/shard_map/ppermute | solution.py:313
  19.1 7.1 %collective-permute-start.8 = (bf16[2,64,256]{2,1,0:T(8,128)(2,1)S(1)}, bf16[2,64,256]{2,1,0:T(8,128)(2,1)S(1)}, u32[]{:S(2)}, u32[]{:S(2)}) collective-permute-start(bf16[2,64,256]{2,1,0:T(8,128)(2,1)S(1)} %turn_leading.1.refs_1_.near), channel_id=1, source_target_pairs={{0,16},{4,20},{8,24},{12,28},{16,0},{20,4},{24,8},{28,12},{1,17},{... | collective-permute-start | bytes 196616 | tf_op jit(solution)/shard_map/ppermute | solution.py:329
  22.3 6.3 %collective-permute-start.9 = (bf16[1,256,256]{2,1,0:T(8,128)(2,1)S(1)}, bf16[1,256,256]{2,1,0:T(8,128)(2,1)S(1)}, u32[]{:S(2)}, u32[]{:S(2)}) collective-permute-start(bf16[1,256,256]{2,1,0:T(8,128)(2,1)S(1)} %get-tuple-element.67.refs_3_), channel_id=1, source_target_pairs={{0,2},{1,3},{2,0},{3,1},{4,6},{5,7},{6,4},{7,5},{8,10},{9,11},{10,... | collective-permute-start | bytes 393224 | tf_op jit(solution)/shard_map/ppermute | solution.py:288
  23.8 9.2 %collective-permute-start.13 = (bf16[2,256,256]{2,1,0:T(8,128)(2,1)S(1)}, bf16[2,256,256]{2,1,0:T(8,128)(2,1)S(1)}, u32[]{:S(2)}, u32[]{:S(2)}) collective-permute-start(bf16[2,256,256]{2,1,0:T(8,128)(2,1)S(1)} %newton.6.refs_1_.refs_4_), channel_id=1, source_target_pairs={{0,1},{1,0},{2,3},{3,2},{4,5},{5,4},{6,7},{7,6},{8,9},{9,8},{10,11... | collective-permute-start | bytes 786440 | tf_op jit(solution)/shard_map/ppermute | solution.py:313
  30.5 4.1 %collective-permute-start.12 = (bf16[1,256,256]{2,1,0:T(8,128)(2,1)S(1)}, bf16[1,256,256]{2,1,0:T(8,128)(2,1)S(1)}, u32[]{:S(2)}, u32[]{:S(2)}) collective-permute-start(bf16[1,256,256]{2,1,0:T(8,128)(2,1)S(1)} %newton.10.refs_3_), channel_id=1, source_target_pairs={{0,1},{1,0},{2,3},{3,2},{4,5},{5,4},{6,7},{7,6},{8,9},{9,8},{10,11... | collective-permute-start | bytes 393224 | tf_op jit(solution)/shard_map/ppermute | solution.py:313
  30.6 10.6 %collective-permute-start.11 = (bf16[2,256,256]{2,1,0:T(8,128)(2,1)S(1)}, bf16[2,256,256]{2,1,0:T(8,128)(2,1)S(1)}, u32[]{:S(2)}, u32[]{:S(2)}) collective-permute-start(bf16[2,256,256]{2,1,0:T(8,128)(2,1)S(1)} %newton.9.refs_1_.refs_2_), channel_id=1, source_target_pairs={{0,1},{1,0},{2,3},{3,2},{4,5},{5,4},{6,7},{7,6},{8,9},{9,8},{10,11... | collective-permute-start | bytes 786440 | tf_op jit(solution)/shard_map/ppermute | solution.py:313
  31.1 10.1 %collective-permute-start.10 = (bf16[2,256,256]{2,1,0:T(8,128)(2,1)S(1)}, bf16[2,256,256]{2,1,0:T(8,128)(2,1)S(1)}, u32[]{:S(2)}, u32[]{:S(2)}) collective-permute-start(bf16[2,256,256]{2,1,0:T(8,128)(2,1)S(1)} %newton.8._.refs_1_), channel_id=1, source_target_pairs={{0,1},{1,0},{2,3},{3,2},{4,5},{5,4},{6,7},{7,6},{8,9},{9,8},{10,11... | collective-permute-start | bytes 786440 | tf_op jit(solution)/shard_map/ppermute | solution.py:313
  31.2 6.0 %collective-permute-start.14 = (bf16[2,2,64,256]{3,2,1,0:T(8,128)(2,1)S(1)}, bf16[2,2,64,256]{3,2,1,0:T(8,128)(2,1)S(1)}, u32[]{:S(2)}, u32[]{:S(2)}) collective-permute-start(bf16[2,2,64,256]{3,2,1,0:T(8,128)(2,1)S(1)} %pair.1.refs_2_.refs_10_), channel_id=1, source_target_pairs={{0,4},{4,0},{8,12},{12,8},{16,20},{20,16},{24,28},{28,24},{1,5},{5... | collective-permute-start | bytes 393224 | tf_op jit(solution)/shard_map/ppermute | solution.py:339
  33.0 6.3 %collective-permute-start.15 = (bf16[2,2,64,256]{3,2,1,0:T(8,128)(2,1)S(1)}, bf16[2,2,64,256]{3,2,1,0:T(8,128)(2,1)S(1)}, u32[]{:S(2)}, u32[]{:S(2)}) collective-permute-start(bf16[2,2,64,256]{3,2,1,0:T(8,128)(2,1)S(1)} %pair.1.refs_2_.refs_10_), channel_id=1, source_target_pairs={{0,8},{4,12},{8,0},{12,4},{16,24},{20,28},{24,16},{28,20},{1,9},{5... | collective-permute-start | bytes 393224 | tf_op jit(solution)/shard_map/ppermute | solution.py:339
  34.6 6.6 %collective-permute-start.16 = (bf16[2,2,64,256]{3,2,1,0:T(8,128)(2,1)S(1)}, bf16[2,2,64,256]{3,2,1,0:T(8,128)(2,1)S(1)}, u32[]{:S(2)}, u32[]{:S(2)}) collective-permute-start(bf16[2,2,64,256]{3,2,1,0:T(8,128)(2,1)S(1)} %pair.1.refs_2_.refs_10_), channel_id=1, source_target_pairs={{0,12},{4,8},{8,4},{12,0},{16,28},{20,24},{24,20},{28,16},{1,13},{... | collective-permute-start | bytes 393224 | tf_op jit(solution)/shard_map/ppermute | solution.py:339
  35.5 5.7 %copy-start = (s32[32]{0:T(128)S(1)}, s32[32]{0:T(128)}, u32[]{:S(2)}) copy-start(s32[32]{0:T(128)} %sources.1) | copy-start | bytes 388

commit v3 on v2

v3 whole, which is shorter than its diff:
```python
import functools

import jax
import jax.numpy as jnp
from jax import lax
from jax.experimental import pallas as pl
from jax.experimental.pallas import tpu as pltpu
from jax.sharding import PartitionSpec as P

MOVE = 2
ITERS = 5
CORES = 2
PIECES = 2
VMEM_LIMIT = 14 * 1024 * 1024
LONG = 1 << 30

f32, bf16, i32 = jnp.float32, jnp.bfloat16, jnp.int32

SMEM = pl.BlockSpec(memory_space=pltpu.SMEM)
VMEM = pl.BlockSpec(memory_space=pltpu.VMEM)
HBM = pl.BlockSpec(memory_space=pltpu.HBM)
ANY = pl.BlockSpec(memory_space=pl.ANY)


def stay(x):
    return pltpu.with_memory_space_constraint(x, pltpu.HBM)


def call(kernel, name, outs, in_specs, out_specs, args, moved=1 << 20, scratch=(), aliases={}):
    return pl.pallas_call(
        kernel,
        out_shape=outs,
        in_specs=in_specs,
        out_specs=out_specs,
        scratch_shapes=scratch,
        input_output_aliases=aliases,
        compiler_params=pltpu.CompilerParams(vmem_limit_bytes=VMEM_LIMIT),
        cost_estimate=pl.CostEstimate(flops=16 * moved if moved == LONG else 0, bytes_accessed=moved, transcendentals=0),
        name=name,
    )(*args)


def assign_slots(bl, ln, first_rows, slot_of_list, plan, crossing):
    blocks, lists = bl.shape[0], slot_of_list.shape[0]
    for l in range(lists):
        slot_of_list[l] = -1

    def visit(b, nxt, wanted):
        l = bl[b]
        s = slot_of_list[l]
        new = jnp.logical_and(s < 0, wanted)
        slot_of_list[l] = jnp.where(new, nxt, s)
        return nxt + new.astype(i32)

    nxt = jnp.int32(0)
    for b in range(MOVE):
        nxt = visit(b, nxt, True)
    for b in range(MOVE, blocks):
        nxt = visit(b, nxt, ln[b] > first_rows)
    crossing[0] = nxt
    for b in range(MOVE, blocks):
        nxt = visit(b, nxt, True)
    plan[blocks] = nxt
    for b in range(blocks):
        plan[b] = slot_of_list[bl[b]]


def gram_kernel(bl_hbm, ln_hbm, points_hbm, targets_hbm, centroids_hbm, plan, crossing, residual, acc, send, *scratch):
    bl, ln, slot_of_list, points, targets, centroids, sems, int_sems = scratch
    blocks, rows, _ = points.shape
    per = acc.shape[0] // CORES
    piece = blocks // PIECES
    copies = [
        pltpu.make_async_copy(bl_hbm, bl, int_sems.at[0]),
        pltpu.make_async_copy(ln_hbm, ln, int_sems.at[1]),
        pltpu.make_async_copy(centroids_hbm, centroids, int_sems.at[2]),
    ]
    for copy in copies:
        copy.start()
    parts = []
    for i in range(PIECES):
        at = pl.ds(i * piece, piece)
        pair = (
            pltpu.make_async_copy(points_hbm.at[at], points.at[at], sems.at[0, i]),
            pltpu.make_async_copy(targets_hbm.at[at], targets.at[at], sems.at[1, i]),
        )
        for copy in pair:
            copy.start()
        parts.append(pair)
    me = lax.axis_index("narrow")
    core = lax.rem(me, CORES)
    acc[...] = jnp.zeros_like(acc)
    copies[0].wait()
    copies[1].wait()
    assign_slots(bl, ln, CORES * rows, slot_of_list, plan, crossing)
    copies[2].wait()
    row_ids = lax.broadcasted_iota(i32, points.shape[1:], 0) + me * rows
    for i in range(PIECES):
        for copy in parts[i]:
            copy.wait()
        for b in range(i * piece, (i + 1) * piece):
            kept = row_ids < ln[b]
            res = jnp.where(kept, points[b].astype(f32) - centroids[pl.ds(bl[b], 1), :], 0.0).astype(bf16)
            residual[b] = res
            slot = plan[b]
            at = lax.div(slot, CORES) + jnp.where(lax.rem(slot, CORES) == core, 0, per)
            acc[at] += lax.dot_general(res, targets[b], (((0,), (0,)), ((), ())), preferred_element_type=f32)
    for i in range(send.shape[0]):
        send[i] = acc[per + i].astype(bf16)


def lead_sum_kernel(per, acc, recv, chip, send):
    lead = recv.shape[0]
    chip[...] = (acc[:lead] + recv[...].astype(f32)).astype(bf16)
    for i in range(send.shape[0]):
        send[i] = acc[per + lead + i].astype(bf16)


def sum_kernel(first, acc, recv, *sums):
    at = 0
    for out in sums:
        count = out.shape[0]
        out[...] = (acc[first + at:first + at + count] + recv[at:at + count].astype(f32)).astype(bf16)
        at += count


def newton_kernel(count, first, offset, extra, gated, acc, recv, *refs):
    pieces, out, chip = refs[:-2], refs[-2], refs[-1]

    def run():
        xs = []
        for i in range(count):
            g = acc[first + i] + recv[offset + i].astype(f32)
            if gated:
                chip[i] = g
            for which in extra:
                piece, row = which[i]
                g = g + pieces[piece][row].astype(f32)
            xs.append(g)
        polar(xs, out)

    if not gated:
        run()
    else:
        plan = refs[-3]
        used = plan[plan.shape[0] - 1] > CORES * first
        pl.when(used)(run)

        @pl.when(jnp.logical_not(used))
        def _():
            out[...] = jnp.zeros_like(out)
            chip[...] = jnp.zeros_like(chip)


def polar(grams, out):
    xs = []
    for g in grams:
        gb = g.astype(bf16)
        p = lax.dot_general(gb, gb, (((1,), (1,)), ((), ())), preferred_element_type=f32)
        scale = lax.rsqrt(jnp.sum(g * g) + 1e-6)
        p = (p * (scale * scale)).astype(bf16)
        xs.append((1.5 * scale) * g - (0.5 * scale) * jnp.dot(p, gb, preferred_element_type=f32))
    for _ in range(ITERS - 1):
        for i, x in enumerate(xs):
            xb = x.astype(bf16)
            p = lax.dot_general(xb, xb, (((1,), (1,)), ((), ())), preferred_element_type=f32).astype(bf16)
            xs[i] = 1.5 * x - 0.5 * jnp.dot(p, xb, preferred_element_type=f32)
    for i, x in enumerate(xs):
        out[i] = x.astype(bf16)


def newton(acc, first, count, recv, offset, crossed, after=(), plan=None, moved=1 << 20):
    extra = [[] for _ in (crossed[0] if crossed else ())]
    flat = []
    for group in crossed:
        for chip, part in enumerate(group):
            extra[chip] += [(len(flat), row) for row in range(part.shape[0])]
            flat.append(part)
    gated = plan is not None
    args = (acc, recv, *flat, *after) + ((plan,) if gated else ())
    specs = [VMEM] * (2 + len(flat)) + [ANY] * len(after) + [SMEM] * gated
    shape = (count,) + acc.shape[1:]
    out = call(
        functools.partial(newton_kernel, count, first, offset, extra, gated),
        "newton",
        (jax.ShapeDtypeStruct(shape, bf16),) + ((jax.ShapeDtypeStruct(shape, f32),) if gated else ()),
        specs,
        (VMEM,) * (1 + gated),
        args,
        moved=moved,
        scratch=[] if gated else [pltpu.VMEM((8, 128), f32)],
    )
    return out if gated else out[0]


def newton_rest_kernel(others, chip, *refs):
    out = refs[-1]
    grams = []
    for i in range(chip.shape[0]):
        g = chip[i]
        for other in refs[:others]:
            g = g + other[i].astype(f32)
        grams.append(g)
    polar(grams, out)


def leading_kernel(plan, residual, own, sibling, out):
    core = lax.rem(lax.axis_index("narrow"), CORES)
    for b in range(MOVE):
        mine = lax.rem(plan[b], CORES) == core
        rotation = jnp.where(mine, own[0], sibling[0])
        out[b] = jnp.dot(residual[b], rotation, preferred_element_type=f32).astype(bf16)


def pair_kernel(near, far, out):
    out[0] = near[...]
    out[1] = far[...]


def place_kernel(hops, blocks, sources, *refs):
    parts, out = refs[:len(hops)], refs[-1]
    here = lax.axis_index("wide")
    for j in range(MOVE):
        donor = lax.div(sources[j], blocks)
        picked = parts[0][0, j]
        for part, group in zip(parts, hops):
            for i, hop in enumerate(group):
                match = donor == (hop if len(parts) == 1 else here ^ hop)
                picked = jnp.where(match, part[i, j], picked)
        out[j] = picked


def turn_kernel(starts, plan, handed, residual, *refs):
    n = len(starts)
    owns, siblings = refs[:n], refs[n:2 * n]
    out, rots, turned, sems = refs[2 * n:]
    blocks, rows, _ = residual.shape
    piece = blocks // PIECES
    core = lax.rem(lax.axis_index("narrow"), CORES)
    for s, o, t in zip(starts, owns, siblings):
        for i in range(o.shape[0]):
            rots[CORES * (s + i) + core] = o[i]
            rots[CORES * (s + i) + 1 - core] = t[i]
    copies = []
    for i in range(PIECES):
        for b in range(i * piece, (i + 1) * piece):
            if b < MOVE:
                turned[b] = handed[b]
            else:
                turned[b] = jnp.dot(residual[b], rots[plan[b]], preferred_element_type=f32).astype(bf16)
        at = pl.ds(i * piece, piece)
        copies.append(pltpu.make_async_copy(turned.at[at], out.at[at], sems.at[i]))
        copies[-1].start()
    for copy in copies:
        copy.wait()


def turn_rest_kernel(first, bl, ln, plan, own, sibling, centroids, points_hbm, _, out, block):
    blocks, rows, _ = points_hbm.shape
    me = lax.axis_index("narrow")
    core = lax.rem(me, CORES)
    row_ids = lax.broadcasted_iota(i32, block.shape, 0) + me * rows

    @pl.loop(MOVE, blocks)
    def _(b):
        @pl.when(plan[b] >= first)
        def _():
            pltpu.sync_copy(points_hbm.at[b], block)
            kept = row_ids < ln[b]
            residual = jnp.where(kept, block[...].astype(f32) - centroids[pl.ds(bl[b], 1), :], 0.0).astype(bf16)
            at = lax.div(plan[b] - first, CORES)
            mine = lax.rem(plan[b], CORES) == core
            rotation = jnp.where(mine, own[at], sibling[at])
            block[...] = jnp.dot(residual, rotation, preferred_element_type=f32).astype(bf16)
            pltpu.sync_copy(block, out.at[b])


def pieces_of(count):
    return [count - count // 2, count // 2] if count > 1 else [count]


def local(wide, narrow, points, targets, centroids, block_list, lengths, sources):
    blocks, rows, width = points.shape
    lists = centroids.shape[0]
    per = lists // CORES
    chips = narrow // CORES
    mat = (width, width)
    lead = MOVE // CORES
    cap = per * 3 // 4 if chips == 2 else per
    rest = per - cap

    plan, crossing, residual, acc, send = call(
        gram_kernel,
        "grams",
        (
            jax.ShapeDtypeStruct((blocks + 1,), i32),
            jax.ShapeDtypeStruct((1,), i32),
            jax.ShapeDtypeStruct(points.shape, bf16),
            jax.ShapeDtypeStruct((lists,) + mat, f32),
            jax.ShapeDtypeStruct((lead,) + mat, bf16),
        ),
        [HBM] * 5,
        (SMEM, SMEM, VMEM, VMEM, VMEM),
        tuple(stay(x) for x in (block_list, lengths, points, targets, centroids)),
        scratch=[
            pltpu.SMEM((blocks,), i32),
            pltpu.SMEM((blocks,), i32),
            pltpu.SMEM((lists,), i32),
            pltpu.VMEM(points.shape, bf16),
            pltpu.VMEM(points.shape, bf16),
            pltpu.VMEM(centroids.shape, f32),
            pltpu.SemaphoreType.DMA((2, PIECES)),
            pltpu.SemaphoreType.DMA((3,)),
        ],
    )

    to_core = [(i, i ^ 1) for i in range(narrow)]
    to_chip = [[(i, (i + CORES * k) % narrow) for i in range(narrow)] for k in range(1, chips)]

    def cross(part):
        return tuple(lax.ppermute(part, "narrow", perm) for perm in to_chip)

    def swap(part):
        return lax.ppermute(part, "narrow", to_core)

    recv = swap(send)
    lead_chip, send_others = call(
        functools.partial(lead_sum_kernel, per),
        "lead_sum",
        (jax.ShapeDtypeStruct((lead,) + mat, bf16), jax.ShapeDtypeStruct((per - lead,) + mat, bf16)),
        [VMEM, VMEM],
        (VMEM, VMEM),
        (acc, recv),
    )
    lead_crossed = cross(lead_chip)
    recv_others = swap(send_others)

    def chip_sums(counts):
        return call(
            functools.partial(sum_kernel, lead),
            "chip_sums",
            tuple(jax.ShapeDtypeStruct((count,) + mat, bf16) for count in counts),
            [VMEM, VMEM],
            (VMEM,) * len(counts),
            (acc, recv_others),
        )

    main_chips = chip_sums(pieces_of(cap - lead))
    main_crossed = [cross(part) for part in main_chips]
    tokens = main_chips
    starts, owns = [0, lead], [None, None]
    if rest:
        starts.append(cap)
        own, rest_chip = newton(acc, cap, rest, recv_others, cap - lead, (), tokens, plan, 1 << 12)
        owns.append(own)
        tokens = (own,)
    owns[0] = newton(acc, 0, lead, recv, 0, (lead_crossed,), tokens)
    siblings = [swap(owns[0])] + [None] * (len(owns) - 1)

    leading = call(
        leading_kernel,
        "turn_leading",
        jax.ShapeDtypeStruct((MOVE, rows, width), bf16),
        [SMEM] + [VMEM] * 3,
        VMEM,
        (plan, residual, owns[0], siblings[0]),
    )
    if wide <= 16 and wide & (wide - 1) == 0:
        half = wide // 2
        far = lax.ppermute(leading, "wide", [(i, i ^ half) for i in range(wide)])
        pair = call(
            pair_kernel,
            "pair",
            jax.ShapeDtypeStruct((2,) + leading.shape, bf16),
            [VMEM, VMEM],
            VMEM,
            (leading, far),
        )
        parts = [pair] + [lax.ppermute(pair, "wide", [(i, i ^ k) for i in range(wide)]) for k in range(1, half)]
        hops = [(k, k ^ half) for k in range(half)]
        token = pair
    else:
        parts = [lax.all_gather(leading, "wide", axis=0)]
        hops = [tuple(range(wide))]
        token = leading

    owns[1] = newton(acc, lead, cap - lead, recv_others, 0, main_crossed, (token,))
    siblings[1:] = [swap(own) for own in owns[1:]]

    handed = call(
        functools.partial(place_kernel, hops, blocks),
        "place",
        jax.ShapeDtypeStruct(leading.shape, bf16),
        [SMEM] + [VMEM] * len(parts) + [ANY],
        VMEM,
        (sources, *parts, owns[1]),
        moved=LONG,
    )
    turned = call(
        functools.partial(turn_kernel, starts),
        "turn",
        pltpu.HBM(points.shape, bf16),
        [SMEM] + [VMEM] * (2 + 2 * len(owns)),
        HBM,
        (plan, handed, residual, *owns, *siblings),
        scratch=[
            pltpu.VMEM((lists,) + mat, bf16),
            pltpu.VMEM(points.shape, bf16),
            pltpu.SemaphoreType.DMA((PIECES,)),
        ],
    )
    if not rest:
        return turned

    def exchange_rest(state):
        crossing, turned, chip = state
        own = call(
            functools.partial(newton_rest_kernel, len(to_chip)),
            "newton_rest",
            jax.ShapeDtypeStruct(chip.shape, bf16),
            [VMEM] * (1 + len(to_chip)),
            VMEM,
            (chip, *cross(chip.astype(bf16))),
        )
        turned = call(
            functools.partial(turn_rest_kernel, CORES * cap),
            "turn_rest",
            pltpu.HBM(turned.shape, bf16),
            [SMEM] * 3 + [VMEM] * 3 + [HBM] * 2,
            HBM,
            (block_list, lengths, plan, own, swap(own), centroids, stay(points), stay(turned)),
            scratch=[pltpu.VMEM((rows, width), bf16)],
            aliases={7: 0},
        )
        return jnp.zeros_like(crossing), turned, own.astype(f32)

    state = (crossing, turned, rest_chip)
    return lax.while_loop(lambda state: state[0][0] > CORES * cap, exchange_rest, state)[1]


def solution(mesh):
    return jax.shard_map(
        functools.partial(local, mesh.shape["wide"], mesh.shape["narrow"]),
        mesh=mesh,
        in_specs=(
            P("wide", "narrow", None),
            P("wide", "narrow", None),
            P("wide", None),
            P("wide"),
            P("wide"),
            P("wide"),
        ),
        out_specs=P("wide", "narrow", None),
        check_vma=False,
    )
```

time: 44.4 us -> 35.4 us (0.80)
  Pallas kernels: 17.3 us -> 11.7 us
  waiting for transfers between devices: 11.4 us -> 7.96 us
  between operations: 0.77 us -> 0.14 us
  loops' own time: 0.01 us -> 0.63 us
    pallas_call x11 -> x10, Pallas kernels: 17.3 us -> 11.7 us  [call(): pl.pallas_call(kernel, out_shape=outs, in_specs=in_specs, out_specs=out_s...]
    ppermute x3, waiting for transfers between devices: 5.72 us -> 1.75 us  [local(): lax.ppermute(pair, 'wide', [(i, i ^ k) for i in range(wide)])]
    ppermute x1, waiting for transfers between devices: 0.24 us -> 3.98 us  [local(): far = lax.ppermute(leading, 'wide', [(i, i ^ half) for i in range(wide)])]
    ppermute x7 -> x5, waiting for transfers between devices: 3.56 us -> 1 us  [swap(): return lax.ppermute(part, 'narrow', to_core)]
    ppermute x4 -> x3, waiting for transfers between devices: 1.9 us -> 1.24 us  [cross(): return tuple((lax.ppermute(part, 'narrow', perm) for perm in to_chip))]
    another operation x1, loops' own time: 0.01 us -> 0.63 us  [local(): lax.while_loop(lambda state: state[0][0] > CORES * cap, exchange_rest, st...]
    ppermute x1, starting transfers between devices: 3.25 us -> 2.66 us  [local(): far = lax.ppermute(leading, 'wide', [(i, i ^ half) for i in range(wide)])]
    ppermute x4 -> x3, starting transfers between devices: 6.48 us -> 6.95 us  [cross(): return tuple((lax.ppermute(part, 'narrow', perm) for perm in to_chip))]
  transfers between devices with their start and end apart: 15 -> 12, of which waited for: 9 -> 5; matrix products, arithmetic and copies ran while one was open for 0% -> 0% of each run, Pallas kernels for 21% -> 17%
where the time goes in v3:
time: 35.4 us; the launch traced here: 35.2 us
  starting transfers between devices  14.8 us (42%)
  Pallas kernels  11.7 us (33%)
  waiting for transfers between devices  7.96 us (22%)
  loops' own time  0.63 us (2%)
    pallas_call x10, Pallas kernels, call(): pl.pallas_call(kernel, out_shape=outs, in_specs=in_specs, out_specs=out_s...  11.7 us
    ppermute x3, starting transfers between devices, cross(): return tuple((lax.ppermute(part, 'narrow', perm) for perm in to_chip))  6.95 us
    ppermute x1, waiting for transfers between devices, local(): far = lax.ppermute(leading, 'wide', [(i, i ^ half) for i in range(wide)])  3.98 us
    ppermute x3, starting transfers between devices, local(): lax.ppermute(pair, 'wide', [(i, i ^ k) for i in range(wide)])  3.55 us
    ppermute x1, starting transfers between devices, local(): far = lax.ppermute(leading, 'wide', [(i, i ^ half) for i in range(wide)])  2.66 us
    ppermute x3, waiting for transfers between devices, local(): lax.ppermute(pair, 'wide', [(i, i ^ k) for i in range(wide)])  1.75 us
    ppermute x5, starting transfers between devices, swap(): return lax.ppermute(part, 'narrow', to_core)  1.6 us
    ppermute x3, waiting for transfers between devices, cross(): return tuple((lax.ppermute(part, 'narrow', perm) for perm in to_chip))  1.24 us
  transfers between devices with their start and end apart: 12, of which 5 were waited for; matrix products, arithmetic and copies ran while one was open for 0% of the time, Pallas kernels for 17%

profile of v3, /device:TPU:0, one launch (start us, length us, event | category | flops | bytes accessed | tf_op | source)
XLA Modules:
  0.0 35.2 jit_solution(8167578475568146557)
XLA Ops:
  0.0 3.4 %grams.1 = (s32[33]{0:T(128)S(1)}, s32[1]{0:T(128)}, bf16[32,64,256]{2,1,0:T(8,128)(2,1)S(1)}, f32[16,256,256]{2,1,0:T(8,128)S(1)}, bf16[1,256,256]{2,1,0:T(8,128)(2,1)S(1)}) custom-call(s32[32]{0:T(128)} %bl_hbm.1, s32[32]{0:T(128)} %ln_hbm.1, bf16[32,64,256]{2,1,0:T(8,128)(2,1)} %points_hbm.1, bf16[32,64,256]{2,1,0:T(8,128)(2,1)} %targets_hbm.1, ...), custom_call_target="tpu_custom_call" | custom-call | bytes 1048576 | tf_op jit(solution)/shard_map/grams/pallas_call | solution.py:30
  3.4 0.5 %collective-permute-start.2 = (bf16[1,256,256]{2,1,0:T(8,128)(2,1)S(1)}, bf16[1,256,256]{2,1,0:T(8,128)(2,1)S(1)}, u32[]{:S(2)}, u32[]{:S(2)}) collective-permute-start(bf16[1,256,256]{2,1,0:T(8,128)(2,1)S(1)} %get-tuple-element.61), channel_id=1, source_target_pairs={{0,1},{1,0},{2,3},{3,2},{4,5},{5,4},{6,7},{7,6},{8,9},{9,8},{10,11... | collective-permute-start | bytes 393224 | tf_op jit(solution)/shard_map/ppermute | solution.py:324
  3.9 1.0 %collective-permute-done.2.recv = bf16[1,256,256]{2,1,0:T(8,128)(2,1)S(1)} collective-permute-done((bf16[1,256,256]{2,1,0:T(8,128)(2,1)S(1)}, bf16[1,256,256]{2,1,0:T(8,128)(2,1)S(1)}, u32[]{:S(2)}, u32[]{:S(2)}) %collective-permute-start.2) | collective-permute-done | bytes 131104 | tf_op jit(solution)/shard_map/ppermute | solution.py:324
  5.0 0.4 %collective-permute-start.4 = (bf16[7,256,256]{2,1,0:T(8,128)(2,1)S(1)}, bf16[7,256,256]{2,1,0:T(8,128)(2,1)S(1)}, u32[]{:S(2)}, u32[]{:S(2)}) collective-permute-start(bf16[7,256,256]{2,1,0:T(8,128)(2,1)S(1)} %get-tuple-element.63), channel_id=1, source_target_pairs={{0,1},{1,0},{2,3},{3,2},{4,5},{5,4},{6,7},{7,6},{8,9},{9,8},{10,11... | collective-permute-start | bytes 2752520 | tf_op jit(solution)/shard_map/ppermute | solution.py:324
  5.4 2.6 %collective-permute-start.3 = (bf16[1,256,256]{2,1,0:T(8,128)(2,1)S(1)}, bf16[1,256,256]{2,1,0:T(8,128)(2,1)S(1)}, u32[]{:S(2)}, u32[]{:S(2)}) collective-permute-start(bf16[1,256,256]{2,1,0:T(8,128)(2,1)S(1)} %get-tuple-element.62), channel_id=1, source_target_pairs={{0,2},{1,3},{2,0},{3,1},{4,6},{5,7},{6,4},{7,5},{8,10},{9,11},{10,... | collective-permute-start | bytes 393224 | tf_op jit(solution)/shard_map/ppermute | solution.py:321
  8.1 0.1 chip_sums.1
  8.2 2.4 %collective-permute-start.10 = (bf16[3,256,256]{2,1,0:T(8,128)(2,1)S(1)}, bf16[3,256,256]{2,1,0:T(8,128)(2,1)S(1)}, u32[]{:S(2)}, u32[]{:S(2)}) collective-permute-start(bf16[3,256,256]{2,1,0:T(8,128)(2,1)S(1)} %get-tuple-element.64.refs_0_), channel_id=1, source_target_pairs={{0,2},{1,3},{2,0},{3,1},{4,6},{5,7},{6,4},{7,5},{8,10},{9,11},{10,... | collective-permute-start | bytes 1179656 | tf_op jit(solution)/shard_map/ppermute | solution.py:321
  10.6 0.6 %newton.3 = (bf16[2,256,256]{2,1,0:T(8,128)(2,1)S(1)}, f32[2,256,256]{2,1,0:T(8,128)S(1)}) custom-call(f32[16,256,256]{2,1,0:T(8,128)S(1)} %get-tuple-element.60.acc, bf16[7,256,256]{2,1,0:T(8,128)(2,1)S(1)} %collective-permute-done.4.recv, bf16[3,256,256]{2,1,0:T(8,128)(2,1)S(1)} %get-tuple-element.64.refs_0_, ...), custom_call_target="tpu_custom_call" | custom-call | bytes 4096 | tf_op jit(solution)/shard_map/newton/pallas_call | solution.py:30
  11.2 1.2 %collective-permute-done.3.refs_0_ = bf16[1,256,256]{2,1,0:T(8,128)(2,1)S(1)} collective-permute-done((bf16[1,256,256]{2,1,0:T(8,128)(2,1)S(1)}, bf16[1,256,256]{2,1,0:T(8,128)(2,1)S(1)}, u32[]{:S(2)}, u32[]{:S(2)}) %collective-permute-start.3) | collective-permute-done | bytes 131104 | tf_op jit(solution)/shard_map/ppermute | solution.py:321
  12.4 1.6 %newton.4.own.refs_0_ = bf16[1,256,256]{2,1,0:T(8,128)(2,1)S(1)} custom-call(f32[16,256,256]{2,1,0:T(8,128)S(1)} %get-tuple-element.60.acc, bf16[1,256,256]{2,1,0:T(8,128)(2,1)S(1)} %collective-permute-done.2.recv, bf16[1,256,256]{2,1,0:T(8,128)(2,1)S(1)} %collective-permute-done.3.refs_0_, bf16[2,256,256]{2,1,0:T(8,128)(2,1)S(1)} %get-tuple-element.66.refs_1_.refs_2_), custom_call_target="tpu_custom_call" | custom-call | bytes 1048576 | tf_op jit(solution)/shard_map/newton/pallas_call | solution.py:30
  14.2 1.9 %collective-permute-start.11 = (bf16[2,256,256]{2,1,0:T(8,128)(2,1)S(1)}, bf16[2,256,256]{2,1,0:T(8,128)(2,1)S(1)}, u32[]{:S(2)}, u32[]{:S(2)}) collective-permute-start(bf16[2,256,256]{2,1,0:T(8,128)(2,1)S(1)} %get-tuple-element.65.refs_1_), channel_id=1, source_target_pairs={{0,2},{1,3},{2,0},{3,1},{4,6},{5,7},{6,4},{7,5},{8,10},{9,11},{10,... | collective-permute-start | bytes 786440 | tf_op jit(solution)/shard_map/ppermute | solution.py:321
  16.1 0.7 %turn_leading.1.near = bf16[2,64,256]{2,1,0:T(8,128)(2,1)S(1)} custom-call(s32[33]{0:T(128)S(1)} %get-tuple-element.98.refs_2_.plan, bf16[32,64,256]{2,1,0:T(8,128)(2,1)S(1)} %get-tuple-element.59.residual, bf16[1,256,256]{2,1,0:T(8,128)(2,1)S(1)} %newton.4.own.refs_0_, bf16[1,256,256]{2,1,0:T(8,128)(2,1)S(1)} %collective-permute-done.5.sibling.refs_3_), custom_call_target="tpu_custom_call" | custom-call | bytes 1048576 | tf_op jit(solution)/shard_map/turn_leading/pallas_call | solution.py:30
  16.8 2.7 %collective-permute-start.6 = (bf16[2,64,256]{2,1,0:T(8,128)(2,1)S(1)}, bf16[2,64,256]{2,1,0:T(8,128)(2,1)S(1)}, u32[]{:S(2)}, u32[]{:S(2)}) collective-permute-start(bf16[2,64,256]{2,1,0:T(8,128)(2,1)S(1)} %turn_leading.1.near), channel_id=1, source_target_pairs={{0,16},{4,20},{8,24},{12,28},{16,0},{20,4},{24,8},{28,12},{1,17},{... | collective-permute-start | bytes 196616 | tf_op jit(solution)/shard_map/ppermute | solution.py:370
  19.5 4.0 %collective-permute-done.6.far = bf16[2,64,256]{2,1,0:T(8,128)(2,1)S(1)} collective-permute-done((bf16[2,64,256]{2,1,0:T(8,128)(2,1)S(1)}, bf16[2,64,256]{2,1,0:T(8,128)(2,1)S(1)}, u32[]{:S(2)}, u32[]{:S(2)}) %collective-permute-start.6) | collective-permute-done | bytes 65568 | tf_op jit(solution)/shard_map/ppermute | solution.py:370
  23.5 1.6 %collective-permute-start.9 = (bf16[2,2,64,256]{3,2,1,0:T(8,128)(2,1)S(1)}, bf16[2,2,64,256]{3,2,1,0:T(8,128)(2,1)S(1)}, u32[]{:S(2)}, u32[]{:S(2)}) collective-permute-start(bf16[2,2,64,256]{3,2,1,0:T(8,128)(2,1)S(1)} %pair.1.refs_2_.refs_0_), channel_id=1, source_target_pairs={{0,12},{4,8},{8,4},{12,0},{16,28},{20,24},{24,20},{28,16},{1,13},{... | collective-permute-start | bytes 393224 | tf_op jit(solution)/shard_map/ppermute | solution.py:379
  25.1 1.5 %collective-permute-start.8 = (bf16[2,2,64,256]{3,2,1,0:T(8,128)(2,1)S(1)}, bf16[2,2,64,256]{3,2,1,0:T(8,128)(2,1)S(1)}, u32[]{:S(2)}, u32[]{:S(2)}) collective-permute-start(bf16[2,2,64,256]{3,2,1,0:T(8,128)(2,1)S(1)} %pair.1.refs_2_.refs_0_), channel_id=1, source_target_pairs={{0,8},{4,12},{8,0},{12,4},{16,24},{20,28},{24,16},{28,20},{1,9},{5... | collective-permute-start | bytes 393224 | tf_op jit(solution)/shard_map/ppermute | solution.py:379
  26.6 0.4 %collective-permute-start.7 = (bf16[2,2,64,256]{3,2,1,0:T(8,128)(2,1)S(1)}, bf16[2,2,64,256]{3,2,1,0:T(8,128)(2,1)S(1)}, u32[]{:S(2)}, u32[]{:S(2)}) collective-permute-start(bf16[2,2,64,256]{3,2,1,0:T(8,128)(2,1)S(1)} %pair.1.refs_2_.refs_0_), channel_id=1, source_target_pairs={{0,4},{4,0},{8,12},{12,8},{16,20},{20,16},{24,28},{28,24},{1,5},{5... | collective-permute-start | bytes 393224 | tf_op jit(solution)/shard_map/ppermute | solution.py:379
  27.0 2.2 %newton.5.refs_4_.refs_1_ = bf16[5,256,256]{2,1,0:T(8,128)(2,1)S(1)} custom-call(f32[16,256,256]{2,1,0:T(8,128)S(1)} %get-tuple-element.60.acc, bf16[7,256,256]{2,1,0:T(8,128)(2,1)S(1)} %collective-permute-done.4.recv, bf16[3,256,256]{2,1,0:T(8,128)(2,1)S(1)} %collective-permute-done.10.refs_0_, bf16[2,256,256]{2,1,0:T(8,128)(2,1)S(1)} %collective-permute-done.11.refs_1_, ...), custom_call_target="tpu_custom_call" | custom-call | bytes 1048576 | tf_op jit(solution)/shard_map/newton/pallas_call | solution.py:30
  29.3 0.6 %collective-permute-start.12 = (bf16[5,256,256]{2,1,0:T(8,128)(2,1)S(1)}, bf16[5,256,256]{2,1,0:T(8,128)(2,1)S(1)}, u32[]{:S(2)}, u32[]{:S(2)}) collective-permute-start(bf16[5,256,256]{2,1,0:T(8,128)(2,1)S(1)} %newton.5.refs_4_.refs_1_), channel_id=1, source_target_pairs={{0,1},{1,0},{2,3},{3,2},{4,5},{5,4},{6,7},{7,6},{8,9},{9,8},{10,11... | collective-permute-start | bytes 1966088 | tf_op jit(solution)/shard_map/ppermute | solution.py:324
  29.9 0.3 collective-permute-done.9.refs_3_
  30.2 1.4 %collective-permute-done.8.refs_2_ = bf16[2,2,64,256]{3,2,1,0:T(8,128)(2,1)S(1)} collective-permute-done((bf16[2,2,64,256]{3,2,1,0:T(8,128)(2,1)S(1)}, bf16[2,2,64,256]{3,2,1,0:T(8,128)(2,1)S(1)}, u32[]{:S(2)}, u32[]{:S(2)}) %collective-permute-start.8) | collective-permute-done | bytes 131104 | tf_op jit(solution)/shard_map/ppermute | solution.py:379
  31.6 0.6 %place.1.handed = bf16[2,64,256]{2,1,0:T(8,128)(2,1)S(1)} custom-call(s32[32]{0:T(128)S(1)} %copy-done, bf16[2,2,64,256]{3,2,1,0:T(8,128)(2,1)S(1)} %pair.1.refs_2_.refs_0_, bf16[2,2,64,256]{3,2,1,0:T(8,128)(2,1)S(1)} %collective-permute-done.7.refs_1_, bf16[2,2,64,256]{3,2,1,0:T(8,128)(2,1)S(1)} %collective-permute-done.8.refs_2_, ...), custom_call_target="tpu_custom_call" | custom-call | flops 17179869184 | bytes 1073741824 | tf_op jit(solution)/shard_map/place/pallas_call | solution.py:30
  32.2 2.3 %turn.1 = bf16[32,64,256]{2,1,0:T(8,128)(2,1)} custom-call(s32[33]{0:T(128)S(1)} %get-tuple-element.98.refs_2_.plan, bf16[2,64,256]{2,1,0:T(8,128)(2,1)S(1)} %place.1.handed, bf16[32,64,256]{2,1,0:T(8,128)(2,1)S(1)} %get-tuple-element.59.residual, bf16[1,256,256]{2,1,0:T(8,128)(2,1)S(1)} %newton.4.own.refs_0_, ...), custom_call_target="tpu_custom_call" | custom-call | bytes 1048576 | tf_op jit(solution)/shard_map/turn/pallas_call | solution.py:30
  34.6 0.6 %while.11 = (s32[1]{0:T(128)}, bf16[32,64,256]{2,1,0:T(8,128)(2,1)}, f32[2,256,256]{2,1,0:T(8,128)S(1)}, s32[32]{0:T(128)S(1)}, s32[32]{0:T(128)S(1)}, /*index=5...) while((s32[1]{0:T(128)}, bf16[32,64,256]{2,1,0:T(8,128)(2,1)}, f32[2,256,256]{2,1,0:T(8,128)S(1)}, ...), condition=%region_1.0_spmd, body=%region_0.0_spmd | while | flops 262145 | bytes 5767329 | solution.py:438
  (19 shorter events, 0.2 us)
Async XLA Ops:
  3.4 1.5 %collective-permute-start.2 = (bf16[1,256,256]{2,1,0:T(8,128)(2,1)S(1)}, bf16[1,256,256]{2,1,0:T(8,128)(2,1)S(1)}, u32[]{:S(2)}, u32[]{:S(2)}) collective-permute-start(bf16[1,256,256]{2,1,0:T(8,128)(2,1)S(1)} %get-tuple-element.61), channel_id=1, source_target_pairs={{0,1},{1,0},{2,3},{3,2},{4,5},{5,4},{6,7},{7,6},{8,9},{9,8},{10,11... | collective-permute-start | bytes 393224 | tf_op jit(solution)/shard_map/ppermute | solution.py:324
  5.0 3.1 %collective-permute-start.4 = (bf16[7,256,256]{2,1,0:T(8,128)(2,1)S(1)}, bf16[7,256,256]{2,1,0:T(8,128)(2,1)S(1)}, u32[]{:S(2)}, u32[]{:S(2)}) collective-permute-start(bf16[7,256,256]{2,1,0:T(8,128)(2,1)S(1)} %get-tuple-element.63), channel_id=1, source_target_pairs={{0,1},{1,0},{2,3},{3,2},{4,5},{5,4},{6,7},{7,6},{8,9},{9,8},{10,11... | collective-permute-start | bytes 2752520 | tf_op jit(solution)/shard_map/ppermute | solution.py:324
  5.4 7.0 %collective-permute-start.3 = (bf16[1,256,256]{2,1,0:T(8,128)(2,1)S(1)}, bf16[1,256,256]{2,1,0:T(8,128)(2,1)S(1)}, u32[]{:S(2)}, u32[]{:S(2)}) collective-permute-start(bf16[1,256,256]{2,1,0:T(8,128)(2,1)S(1)} %get-tuple-element.62), channel_id=1, source_target_pairs={{0,2},{1,3},{2,0},{3,1},{4,6},{5,7},{6,4},{7,5},{8,10},{9,11},{10,... | collective-permute-start | bytes 393224 | tf_op jit(solution)/shard_map/ppermute | solution.py:321
  8.2 18.8 %collective-permute-start.10 = (bf16[3,256,256]{2,1,0:T(8,128)(2,1)S(1)}, bf16[3,256,256]{2,1,0:T(8,128)(2,1)S(1)}, u32[]{:S(2)}, u32[]{:S(2)}) collective-permute-start(bf16[3,256,256]{2,1,0:T(8,128)(2,1)S(1)} %get-tuple-element.64.refs_0_), channel_id=1, source_target_pairs={{0,2},{1,3},{2,0},{3,1},{4,6},{5,7},{6,4},{7,5},{8,10},{9,11},{10,... | collective-permute-start | bytes 1179656 | tf_op jit(solution)/shard_map/ppermute | solution.py:321
  14.1 17.5 %copy-start = (s32[32]{0:T(128)S(1)}, s32[32]{0:T(128)}, u32[]{:S(2)}) copy-start(s32[32]{0:T(128)} %sources.1) | copy-start | bytes 388
  14.1 2.0 %collective-permute-start.5 = (bf16[1,256,256]{2,1,0:T(8,128)(2,1)S(1)}, bf16[1,256,256]{2,1,0:T(8,128)(2,1)S(1)}, u32[]{:S(2)}, u32[]{:S(2)}) collective-permute-start(bf16[1,256,256]{2,1,0:T(8,128)(2,1)S(1)} %newton.4.own.refs_0_), channel_id=1, source_target_pairs={{0,1},{1,0},{2,3},{3,2},{4,5},{5,4},{6,7},{7,6},{8,9},{9,8},{10,11... | collective-permute-start | bytes 393224 | tf_op jit(solution)/shard_map/ppermute | solution.py:324
  14.2 12.9 %collective-permute-start.11 = (bf16[2,256,256]{2,1,0:T(8,128)(2,1)S(1)}, bf16[2,256,256]{2,1,0:T(8,128)(2,1)S(1)}, u32[]{:S(2)}, u32[]{:S(2)}) collective-permute-start(bf16[2,256,256]{2,1,0:T(8,128)(2,1)S(1)} %get-tuple-element.65.refs_1_), channel_id=1, source_target_pairs={{0,2},{1,3},{2,0},{3,1},{4,6},{5,7},{6,4},{7,5},{8,10},{9,11},{10,... | collective-permute-start | bytes 786440 | tf_op jit(solution)/shard_map/ppermute | solution.py:321
  16.8 6.6 %collective-permute-start.6 = (bf16[2,64,256]{2,1,0:T(8,128)(2,1)S(1)}, bf16[2,64,256]{2,1,0:T(8,128)(2,1)S(1)}, u32[]{:S(2)}, u32[]{:S(2)}) collective-permute-start(bf16[2,64,256]{2,1,0:T(8,128)(2,1)S(1)} %turn_leading.1.near), channel_id=1, source_target_pairs={{0,16},{4,20},{8,24},{12,28},{16,0},{20,4},{24,8},{28,12},{1,17},{... | collective-permute-start | bytes 196616 | tf_op jit(solution)/shard_map/ppermute | solution.py:370
  23.5 6.7 %collective-permute-start.9 = (bf16[2,2,64,256]{3,2,1,0:T(8,128)(2,1)S(1)}, bf16[2,2,64,256]{3,2,1,0:T(8,128)(2,1)S(1)}, u32[]{:S(2)}, u32[]{:S(2)}) collective-permute-start(bf16[2,2,64,256]{3,2,1,0:T(8,128)(2,1)S(1)} %pair.1.refs_2_.refs_0_), channel_id=1, source_target_pairs={{0,12},{4,8},{8,4},{12,0},{16,28},{20,24},{24,20},{28,16},{1,13},{... | collective-permute-start | bytes 393224 | tf_op jit(solution)/shard_map/ppermute | solution.py:379
  25.1 6.5 %collective-permute-start.8 = (bf16[2,2,64,256]{3,2,1,0:T(8,128)(2,1)S(1)}, bf16[2,2,64,256]{3,2,1,0:T(8,128)(2,1)S(1)}, u32[]{:S(2)}, u32[]{:S(2)}) collective-permute-start(bf16[2,2,64,256]{3,2,1,0:T(8,128)(2,1)S(1)} %pair.1.refs_2_.refs_0_), channel_id=1, source_target_pairs={{0,8},{4,12},{8,0},{12,4},{16,24},{20,28},{24,16},{28,20},{1,9},{5... | collective-permute-start | bytes 393224 | tf_op jit(solution)/shard_map/ppermute | solution.py:379
  26.6 5.0 %collective-permute-start.7 = (bf16[2,2,64,256]{3,2,1,0:T(8,128)(2,1)S(1)}, bf16[2,2,64,256]{3,2,1,0:T(8,128)(2,1)S(1)}, u32[]{:S(2)}, u32[]{:S(2)}) collective-permute-start(bf16[2,2,64,256]{3,2,1,0:T(8,128)(2,1)S(1)} %pair.1.refs_2_.refs_0_), channel_id=1, source_target_pairs={{0,4},{4,0},{8,12},{12,8},{16,20},{20,16},{24,28},{28,24},{1,5},{5... | collective-permute-start | bytes 393224 | tf_op jit(solution)/shard_map/ppermute | solution.py:379
  27.0 5.2 %collective-permute-start.13 = (bf16[2,256,256]{2,1,0:T(8,128)(2,1)S(1)}, bf16[2,256,256]{2,1,0:T(8,128)(2,1)S(1)}, u32[]{:S(2)}, u32[]{:S(2)}) collective-permute-start(bf16[2,256,256]{2,1,0:T(8,128)(2,1)S(1)} %get-tuple-element.66.refs_1_.refs_2_), channel_id=1, source_target_pairs={{0,1},{1,0},{2,3},{3,2},{4,5},{5,4},{6,7},{7,6},{8,9},{9,8},{10,11... | collective-permute-start | bytes 786440 | tf_op jit(solution)/shard_map/ppermute | solution.py:324
  29.3 3.0 %collective-permute-start.12 = (bf16[5,256,256]{2,1,0:T(8,128)(2,1)S(1)}, bf16[5,256,256]{2,1,0:T(8,128)(2,1)S(1)}, u32[]{:S(2)}, u32[]{:S(2)}) collective-permute-start(bf16[5,256,256]{2,1,0:T(8,128)(2,1)S(1)} %newton.5.refs_4_.refs_1_), channel_id=1, source_target_pairs={{0,1},{1,0},{2,3},{3,2},{4,5},{5,4},{6,7},{7,6},{8,9},{9,8},{10,11... | collective-permute-start | bytes 1966088 | tf_op jit(solution)/shard_map/ppermute | solution.py:324
  32.2 2.4 %copy-start.1 = (f32[16,256]{1,0:T(8,128)S(1)}, f32[16,256]{1,0:T(8,128)}, u32[]{:S(2)}) copy-start(f32[16,256]{1,0:T(8,128)} %centroids_hbm.1) | copy-start | bytes 49156
  32.2 2.4 %copy-start.2 = (s32[32]{0:T(128)S(1)}, s32[32]{0:T(128)}, u32[]{:S(2)}) copy-start(s32[32]{0:T(128)} %bl_hbm.1) | copy-start | bytes 388
  32.2 2.4 %copy-start.3 = (s32[32]{0:T(128)S(1)}, s32[32]{0:T(128)}, u32[]{:S(2)}) copy-start(s32[32]{0:T(128)} %ln_hbm.1) | copy-start | bytes 388

commit v4 on v3

--- a/solution.py
+++ b/solution.py
@@ -13,6 +13,9 @@
 PIECES = 2
 VMEM_LIMIT = 14 * 1024 * 1024
 LONG = 1 << 30
+GROUP = 4
+LEAD_FLOPS = 2800000000
+PAIR_FLOPS = 0
 
 f32, bf16, i32 = jnp.float32, jnp.bfloat16, jnp.int32
 
@@ -26,7 +29,7 @@
     return pltpu.with_memory_space_constraint(x, pltpu.HBM)
 
 
-def call(kernel, name, outs, in_specs, out_specs, args, moved=1 << 20, scratch=(), aliases={}):
+def call(kernel, name, outs, in_specs, out_specs, args, moved=1 << 20, flops=0, scratch=(), aliases={}):
     return pl.pallas_call(
         kernel,
         out_shape=outs,
@@ -35,7 +38,7 @@
         scratch_shapes=scratch,
         input_output_aliases=aliases,
         compiler_params=pltpu.CompilerParams(vmem_limit_bytes=VMEM_LIMIT),
-        cost_estimate=pl.CostEstimate(flops=16 * moved if moved == LONG else 0, bytes_accessed=moved, transcendentals=0),
+        cost_estimate=pl.CostEstimate(flops=16 * moved if moved == LONG else flops, bytes_accessed=moved, transcendentals=0),
         name=name,
     )(*args)
 
@@ -65,8 +68,8 @@
         plan[b] = slot_of_list[bl[b]]
 
 
-def gram_kernel(bl_hbm, ln_hbm, points_hbm, targets_hbm, centroids_hbm, plan, crossing, residual, acc, send, *scratch):
-    bl, ln, slot_of_list, points, targets, centroids, sems, int_sems = scratch
+def gram_kernel(bl_hbm, ln_hbm, sources_hbm, points_hbm, targets_hbm, centroids_hbm, plan, crossing, residual, same, acc, send, *scratch):
+    bl, ln, sources, slot_of_list, points, targets, centroids, sems, int_sems = scratch
     blocks, rows, _ = points.shape
     per = acc.shape[0] // CORES
     piece = blocks // PIECES
@@ -74,6 +77,7 @@
         pltpu.make_async_copy(bl_hbm, bl, int_sems.at[0]),
         pltpu.make_async_copy(ln_hbm, ln, int_sems.at[1]),
         pltpu.make_async_copy(centroids_hbm, centroids, int_sems.at[2]),
+        pltpu.make_async_copy(sources_hbm, sources, int_sems.at[3]),
     ]
     for copy in copies:
         copy.start()
@@ -94,6 +98,11 @@
     copies[1].wait()
     assign_slots(bl, ln, CORES * rows, slot_of_list, plan, crossing)
     copies[2].wait()
+    copies[3].wait()
+    for j in range(MOVE):
+        plan[blocks + 1 + j] = lax.div(sources[j], blocks)
+        mine = lax.rem(plan[j], CORES) == core
+        same[j] = jnp.full(same.shape[1:], jnp.where(mine, 1.0, 0.0), f32)
     row_ids = lax.broadcasted_iota(i32, points.shape[1:], 0) + me * rows
     for i in range(PIECES):
         for copy in parts[i]:
@@ -143,7 +152,7 @@
         run()
     else:
         plan = refs[-3]
-        used = plan[plan.shape[0] - 1] > CORES * first
+        used = plan[plan.shape[0] - 1 - MOVE] > CORES * first
         pl.when(used)(run)
 
         @pl.when(jnp.logical_not(used))
@@ -204,11 +213,9 @@
     polar(grams, out)
 
 
-def leading_kernel(plan, residual, own, sibling, out):
-    core = lax.rem(lax.axis_index("narrow"), CORES)
+def leading_kernel(same, residual, own, sibling, out):
     for b in range(MOVE):
-        mine = lax.rem(plan[b], CORES) == core
-        rotation = jnp.where(mine, own[0], sibling[0])
+        rotation = jnp.where(same[b, :1] > 0.5, own[0], sibling[0])
         out[b] = jnp.dot(residual[b], rotation, preferred_element_type=f32).astype(bf16)
 
 
@@ -217,37 +224,46 @@
     out[1] = far[...]
 
 
-def place_kernel(hops, blocks, sources, *refs):
-    parts, out = refs[:len(hops)], refs[-1]
-    here = lax.axis_index("wide")
-    for j in range(MOVE):
-        donor = lax.div(sources[j], blocks)
-        picked = parts[0][0, j]
-        for part, group in zip(parts, hops):
-            for i, hop in enumerate(group):
-                match = donor == (hop if len(parts) == 1 else here ^ hop)
-                picked = jnp.where(match, part[i, j], picked)
-        out[j] = picked
-
-
-def turn_kernel(starts, plan, handed, residual, *refs):
-    n = len(starts)
-    owns, siblings = refs[:n], refs[n:2 * n]
-    out, rots, turned, sems = refs[2 * n:]
+def arrived_kernel(*refs):
+    refs[-1][...] = jnp.zeros_like(refs[-1])
+
+
+def gather_kernel(starts, n_own, *refs):
+    owns, siblings, rots = refs[:n_own], refs[n_own:-1], refs[-1]
+    core = lax.rem(lax.axis_index("narrow"), CORES)
+    for s, own in zip(starts, owns):
+        for i in range(own.shape[0]):
+            rots[CORES * (s + i) + core] = own[i]
+    for s, sibling in zip(starts, siblings):
+        for i in range(sibling.shape[0]):
+            rots[CORES * (s + i) + 1 - core] = sibling[i]
+
+
+def turn_kernel(first, hops, plan_hbm, residual, main, _, *refs):
+    parts = refs[:len(hops)]
+    out, rots, plan, turned, sems, plan_sem = refs[-6:]
     blocks, rows, _ = residual.shape
     piece = blocks // PIECES
     core = lax.rem(lax.axis_index("narrow"), CORES)
-    for s, o, t in zip(starts, owns, siblings):
-        for i in range(o.shape[0]):
-            rots[CORES * (s + i) + core] = o[i]
-            rots[CORES * (s + i) + 1 - core] = t[i]
+    here = lax.axis_index("wide")
+    fetch = pltpu.make_async_copy(plan_hbm, plan, plan_sem)
+    fetch.start()
+    for i in range(main.shape[0]):
+        rots[CORES * (first + i) + 1 - core] = main[i]
+    fetch.wait()
     copies = []
-    for i in range(PIECES):
-        for b in range(i * piece, (i + 1) * piece):
-            if b < MOVE:
-                turned[b] = handed[b]
-            else:
+    for i in reversed(range(PIECES)):
+        for b in reversed(range(i * piece, (i + 1) * piece)):
+            if b >= MOVE:
                 turned[b] = jnp.dot(residual[b], rots[plan[b]], preferred_element_type=f32).astype(bf16)
+                continue
+            donor = plan[blocks + 1 + b]
+            picked = parts[0][0, b]
+            for part, group in zip(parts, hops):
+                for k, hop in enumerate(group):
+                    match = donor == (hop if len(parts) == 1 else here ^ hop)
+                    picked = jnp.where(match, part[k, b], picked)
+            turned[b] = picked
         at = pl.ds(i * piece, piece)
         copies.append(pltpu.make_async_copy(turned.at[at], out.at[at], sems.at[i]))
         copies[-1].start()
@@ -276,7 +292,7 @@
 
 
 def pieces_of(count):
-    return [count - count // 2, count // 2] if count > 1 else [count]
+    return [count]
 
 
 def local(wide, narrow, points, targets, centroids, block_list, lengths, sources):
@@ -289,20 +305,22 @@
     cap = per * 3 // 4 if chips == 2 else per
     rest = per - cap
 
-    plan, crossing, residual, acc, send = call(
+    plan, crossing, residual, same, acc, send = call(
         gram_kernel,
         "grams",
         (
-            jax.ShapeDtypeStruct((blocks + 1,), i32),
+            jax.ShapeDtypeStruct((blocks + 1 + MOVE,), i32),
             jax.ShapeDtypeStruct((1,), i32),
             jax.ShapeDtypeStruct(points.shape, bf16),
+            jax.ShapeDtypeStruct((MOVE, 8, width), f32),
             jax.ShapeDtypeStruct((lists,) + mat, f32),
             jax.ShapeDtypeStruct((lead,) + mat, bf16),
         ),
-        [HBM] * 5,
-        (SMEM, SMEM, VMEM, VMEM, VMEM),
-        tuple(stay(x) for x in (block_list, lengths, points, targets, centroids)),
+        [HBM] * 6,
+        (SMEM, SMEM, VMEM, VMEM, VMEM, VMEM),
+        tuple(stay(x) for x in (block_list, lengths, sources, points, targets, centroids)),
         scratch=[
+            pltpu.SMEM((blocks,), i32),
             pltpu.SMEM((blocks,), i32),
             pltpu.SMEM((blocks,), i32),
             pltpu.SMEM((lists,), i32),
@@ -310,7 +328,7 @@
             pltpu.VMEM(points.shape, bf16),
             pltpu.VMEM(centroids.shape, f32),
             pltpu.SemaphoreType.DMA((2, PIECES)),
-            pltpu.SemaphoreType.DMA((3,)),
+            pltpu.SemaphoreType.DMA((4,)),
         ],
     )
 
@@ -348,22 +366,25 @@
     main_chips = chip_sums(pieces_of(cap - lead))
     main_crossed = [cross(part) for part in main_chips]
     tokens = main_chips
-    starts, owns = [0, lead], [None, None]
+    starts, owns = [0], []
     if rest:
         starts.append(cap)
-        own, rest_chip = newton(acc, cap, rest, recv_others, cap - lead, (), tokens, plan, 1 << 12)
-        owns.append(own)
-        tokens = (own,)
-    owns[0] = newton(acc, 0, lead, recv, 0, (lead_crossed,), tokens)
-    siblings = [swap(owns[0])] + [None] * (len(owns) - 1)
+        overflow = crossing[0] > CORES * cap
+        tokens = (*tokens, overflow.astype(i32).reshape(1))
+        rest_own, rest_chip = newton(acc, cap, rest, recv_others, cap - lead, (), tokens, plan, 1 << 12)
+        owns.append(rest_own)
+        tokens = (rest_own,)
+    owns.insert(0, newton(acc, 0, lead, recv, 0, (lead_crossed,), tokens))
+    siblings = [swap(owns[0])]
 
     leading = call(
         leading_kernel,
         "turn_leading",
         jax.ShapeDtypeStruct((MOVE, rows, width), bf16),
-        [SMEM] + [VMEM] * 3,
+        [VMEM] * 4,
         VMEM,
-        (plan, residual, owns[0], siblings[0]),
+        (same, residual, owns[0], siblings[0]),
+        flops=LEAD_FLOPS,
     )
     if wide <= 16 and wide & (wide - 1) == 0:
         half = wide // 2
@@ -375,45 +396,57 @@
             [VMEM, VMEM],
             VMEM,
             (leading, far),
+            flops=PAIR_FLOPS,
         )
-        parts = [pair] + [lax.ppermute(pair, "wide", [(i, i ^ k) for i in range(wide)]) for k in range(1, half)]
-        hops = [(k, k ^ half) for k in range(half)]
+        order = range(1, half)
+        parts = [pair] + [lax.ppermute(pair, "wide", [(i, i ^ k) for i in range(wide)]) for k in order]
+        hops = [(k, k ^ half) for k in [0, *order]]
         token = pair
     else:
         parts = [lax.all_gather(leading, "wide", axis=0)]
         hops = [tuple(range(wide))]
         token = leading
-
-    owns[1] = newton(acc, lead, cap - lead, recv_others, 0, main_crossed, (token,))
-    siblings[1:] = [swap(own) for own in owns[1:]]
-
-    handed = call(
-        functools.partial(place_kernel, hops, blocks),
-        "place",
-        jax.ShapeDtypeStruct(leading.shape, bf16),
-        [SMEM] + [VMEM] * len(parts) + [ANY],
+    main = newton(acc, lead, cap - lead, recv_others, 0, main_crossed, (token,))
+    siblings += [swap(own) for own in owns[1:]]
+    other = swap(main)
+
+    rots = call(
+        functools.partial(gather_kernel, starts + [lead], len(owns) + 1),
+        "gather_rotations",
+        jax.ShapeDtypeStruct((lists,) + mat, bf16),
+        [VMEM] * (1 + len(owns) + len(siblings)),
         VMEM,
-        (sources, *parts, owns[1]),
+        (*owns, main, *siblings),
+    )
+    token = call(
+        arrived_kernel,
+        "arrived",
+        jax.ShapeDtypeStruct((8, 128), f32),
+        [ANY] * (1 + len(parts)),
+        VMEM,
+        (*parts, rots),
         moved=LONG,
     )
-    turned = call(
-        functools.partial(turn_kernel, starts),
+    turned, _ = call(
+        functools.partial(turn_kernel, lead, hops),
         "turn",
-        pltpu.HBM(points.shape, bf16),
-        [SMEM] + [VMEM] * (2 + 2 * len(owns)),
-        HBM,
-        (plan, handed, residual, *owns, *siblings),
+        (pltpu.HBM(points.shape, bf16), jax.ShapeDtypeStruct(rots.shape, bf16)),
+        [ANY] + [VMEM] * (3 + len(parts)) + [ANY],
+        (HBM, VMEM),
+        (plan, residual, other, rots, *parts, token),
         scratch=[
-            pltpu.VMEM((lists,) + mat, bf16),
+            pltpu.SMEM(plan.shape, i32),
             pltpu.VMEM(points.shape, bf16),
             pltpu.SemaphoreType.DMA((PIECES,)),
+            pltpu.SemaphoreType.DMA(()),
         ],
+        aliases={3: 1},
     )
     if not rest:
         return turned
 
     def exchange_rest(state):
-        crossing, turned, chip = state
+        turned, chip = state
         own = call(
             functools.partial(newton_rest_kernel, len(to_chip)),
             "newton_rest",
@@ -432,10 +465,9 @@
             scratch=[pltpu.VMEM((rows, width), bf16)],
             aliases={7: 0},
         )
-        return jnp.zeros_like(crossing), turned, own.astype(f32)
-
-    state = (crossing, turned, rest_chip)
-    return lax.while_loop(lambda state: state[0][0] > CORES * cap, exchange_rest, state)[1]
+        return turned
+
+    return lax.cond(overflow, exchange_rest, lambda state: state[0], (turned, rest_chip))
 
 
 def solution(mesh):

time: 35.4 us -> 35 us (0.989)
  starting transfers between devices: 14.8 us -> 12.8 us
  Pallas kernels: 11.7 us -> 12.5 us
  waiting for transfers between devices: 7.96 us -> 8.76 us
  between operations: 0.14 us -> 0.79 us
  loops' own time: 0.63 us -> 0.01 us
    ppermute x3 -> x2, starting transfers between devices: 6.95 us -> 5.02 us  [cross(): return tuple((lax.ppermute(part, 'narrow', perm) for perm in to_chip))]
    ppermute x3 -> x2, waiting for transfers between devices: 1.24 us -> 0.01 us  [cross(): return tuple((lax.ppermute(part, 'narrow', perm) for perm in to_chip))]
    ppermute x3, waiting for transfers between devices: 1.75 us -> 2.94 us  [local(): lax.ppermute(pair, 'wide', [(i, i ^ k) for i in range(wide)])]
    ppermute x5, waiting for transfers between devices: 1 us -> 1.83 us  [swap(): return lax.ppermute(part, 'narrow', to_core)]
    pallas_call x10 -> x11, Pallas kernels: 11.7 us -> 12.5 us  [call(): pl.pallas_call(kernel, out_shape=outs, in_specs=in_specs, out_specs=out_s...]
    another operation x1, loops' own time: 0.63 us -> 0.01 us  [local(): lax.cond(overflow, exchange_rest, lambda state: state[0], (turned, rest_c...]
  transfers between devices with their start and end apart: 12 -> 11, of which waited for: 5 -> 5; matrix products, arithmetic and copies ran while one was open for 0% -> 0% of each run, Pallas kernels for 17% -> 19%
where the time goes in v4:
time: 35 us; the launch traced here: 34.9 us
  starting transfers between devices  12.8 us (37%)
  Pallas kernels  12.5 us (36%)
  waiting for transfers between devices  8.76 us (25%)
  between operations  0.79 us (2%)
    pallas_call x11, Pallas kernels, call(): pl.pallas_call(kernel, out_shape=outs, in_specs=in_specs, out_specs=out_s...  12.5 us
    ppermute x2, starting transfers between devices, cross(): return tuple((lax.ppermute(part, 'narrow', perm) for perm in to_chip))  5.02 us
    ppermute x1, waiting for transfers between devices, local(): far = lax.ppermute(leading, 'wide', [(i, i ^ half) for i in range(wide)])  3.98 us
    ppermute x3, starting transfers between devices, local(): lax.ppermute(pair, 'wide', [(i, i ^ k) for i in range(wide)])  3.55 us
    ppermute x3, waiting for transfers between devices, local(): lax.ppermute(pair, 'wide', [(i, i ^ k) for i in range(wide)])  2.94 us
    ppermute x1, starting transfers between devices, local(): far = lax.ppermute(leading, 'wide', [(i, i ^ half) for i in range(wide)])  2.65 us
    ppermute x5, waiting for transfers between devices, swap(): return lax.ppermute(part, 'narrow', to_core)  1.83 us
    ppermute x5, starting transfers between devices, swap(): return lax.ppermute(part, 'narrow', to_core)  1.59 us
  transfers between devices with their start and end apart: 11, of which 5 were waited for; matrix products, arithmetic and copies ran while one was open for 0% of the time, Pallas kernels for 19%

profile of v4, /device:TPU:0, one launch (start us, length us, event | category | flops | bytes accessed | tf_op | source)
XLA Modules:
  0.0 34.9 jit_solution(5854986055968823508)
XLA Ops:
  0.0 3.4 %grams.1 = (s32[35]{0:T(128)S(1)}, s32[1]{0:T(128)}, bf16[32,64,256]{2,1,0:T(8,128)(2,1)S(1)}, f32[2,8,256]{2,1,0:T(8,128)S(1)}, f32[16,256,256]{2,1,0:T(8,128)S(1)}, /*index=5*/bf16[1,256,256]{2,1,0:T(8,128)(2,1)S(1)}) custom-call(s32[32]{0:T(128)} %bl_hbm.1, s32[32]{0:T(128)} %ln_hbm.1, s32[32]{0:T(128)} %sources_hbm.1, bf16[32,64,256]{2,1,0:T(8,128)(2,1)} %points_hbm.1, ...), custom_call_target="tpu_custom_call" | custom-call | bytes 1048576 | tf_op jit(solution)/shard_map/grams/pallas_call | solution.py:33
  3.4 0.5 %collective-permute-start.2 = (bf16[1,256,256]{2,1,0:T(8,128)(2,1)S(1)}, bf16[1,256,256]{2,1,0:T(8,128)(2,1)S(1)}, u32[]{:S(2)}, u32[]{:S(2)}) collective-permute-start(bf16[1,256,256]{2,1,0:T(8,128)(2,1)S(1)} %get-tuple-element.45), channel_id=1, source_target_pairs={{0,1},{1,0},{2,3},{3,2},{4,5},{5,4},{6,7},{7,6},{8,9},{9,8},{10,11... | collective-permute-start | bytes 393224 | tf_op jit(solution)/shard_map/ppermute | solution.py:342
  3.9 1.0 %collective-permute-done.2.recv = bf16[1,256,256]{2,1,0:T(8,128)(2,1)S(1)} collective-permute-done((bf16[1,256,256]{2,1,0:T(8,128)(2,1)S(1)}, bf16[1,256,256]{2,1,0:T(8,128)(2,1)S(1)}, u32[]{:S(2)}, u32[]{:S(2)}) %collective-permute-start.2) | collective-permute-done | bytes 131104 | tf_op jit(solution)/shard_map/ppermute | solution.py:342
  4.9 0.1 lead_sum.1
  5.0 0.4 %collective-permute-start.3 = (bf16[7,256,256]{2,1,0:T(8,128)(2,1)S(1)}, bf16[7,256,256]{2,1,0:T(8,128)(2,1)S(1)}, u32[]{:S(2)}, u32[]{:S(2)}) collective-permute-start(bf16[7,256,256]{2,1,0:T(8,128)(2,1)S(1)} %get-tuple-element.46), channel_id=1, source_target_pairs={{0,1},{1,0},{2,3},{3,2},{4,5},{5,4},{6,7},{7,6},{8,9},{9,8},{10,11... | collective-permute-start | bytes 2752520 | tf_op jit(solution)/shard_map/ppermute | solution.py:342
  5.5 2.7 %collective-permute-start.5 = (bf16[1,256,256]{2,1,0:T(8,128)(2,1)S(1)}, bf16[1,256,256]{2,1,0:T(8,128)(2,1)S(1)}, u32[]{:S(2)}, u32[]{:S(2)}) collective-permute-start(bf16[1,256,256]{2,1,0:T(8,128)(2,1)S(1)} %get-tuple-element.48), channel_id=1, source_target_pairs={{0,2},{1,3},{2,0},{3,1},{4,6},{5,7},{6,4},{7,5},{8,10},{9,11},{10,... | collective-permute-start | bytes 393224 | tf_op jit(solution)/shard_map/ppermute | solution.py:339
  8.1 0.1 chip_sums.1.refs_0_
  8.2 2.4 %collective-permute-start.4 = (bf16[5,256,256]{2,1,0:T(8,128)(2,1)S(1)}, bf16[5,256,256]{2,1,0:T(8,128)(2,1)S(1)}, u32[]{:S(2)}, u32[]{:S(2)}) collective-permute-start(bf16[5,256,256]{2,1,0:T(8,128)(2,1)S(1)} %chip_sums.1.refs_0_), channel_id=1, source_target_pairs={{0,2},{1,3},{2,0},{3,1},{4,6},{5,7},{6,4},{7,5},{8,10},{9,11},{10,... | collective-permute-start | bytes 1966088 | tf_op jit(solution)/shard_map/ppermute | solution.py:339
  11.3 2.5 %newton.3 = (bf16[2,256,256]{2,1,0:T(8,128)(2,1)S(1)}, f32[2,256,256]{2,1,0:T(8,128)S(1)}) custom-call(f32[16,256,256]{2,1,0:T(8,128)S(1)} %get-tuple-element.44.acc, bf16[7,256,256]{2,1,0:T(8,128)(2,1)S(1)} %collective-permute-done.3.recv, bf16[5,256,256]{2,1,0:T(8,128)(2,1)S(1)} %chip_sums.1.refs_0_, s32[1]{0:T(128)} %convert_element_type.10.refs_1_, ...), custom_call_target="tpu_custom_call" | custom-call | bytes 4096 | tf_op jit(solution)/shard_map/newton/pallas_call | solution.py:33
  13.8 1.6 %newton.4.own.refs_0_ = bf16[1,256,256]{2,1,0:T(8,128)(2,1)S(1)} custom-call(f32[16,256,256]{2,1,0:T(8,128)S(1)} %get-tuple-element.44.acc, bf16[1,256,256]{2,1,0:T(8,128)(2,1)S(1)} %collective-permute-done.2.recv, bf16[1,256,256]{2,1,0:T(8,128)(2,1)S(1)} %collective-permute-done.5.refs_0_, bf16[2,256,256]{2,1,0:T(8,128)(2,1)S(1)} %get-tuple-element.49.refs_1_), custom_call_target="tpu_custom_call" | custom-call | bytes 1048576 | tf_op jit(solution)/shard_map/newton/pallas_call | solution.py:33
  15.4 0.1 collective-permute-start.6
  15.5 0.5 %collective-permute-start.9 = (bf16[2,256,256]{2,1,0:T(8,128)(2,1)S(1)}, bf16[2,256,256]{2,1,0:T(8,128)(2,1)S(1)}, u32[]{:S(2)}, u32[]{:S(2)}) collective-permute-start(bf16[2,256,256]{2,1,0:T(8,128)(2,1)S(1)} %get-tuple-element.49.refs_1_), channel_id=1, source_target_pairs={{0,1},{1,0},{2,3},{3,2},{4,5},{5,4},{6,7},{7,6},{8,9},{9,8},{10,11... | collective-permute-start | bytes 786440 | tf_op jit(solution)/shard_map/ppermute | solution.py:342
  16.0 0.8 %collective-permute-done.6.sibling.refs_3_ = bf16[1,256,256]{2,1,0:T(8,128)(2,1)S(1)} collective-permute-done((bf16[1,256,256]{2,1,0:T(8,128)(2,1)S(1)}, bf16[1,256,256]{2,1,0:T(8,128)(2,1)S(1)}, u32[]{:S(2)}, u32[]{:S(2)}) %collective-permute-start.6) | collective-permute-done | bytes 131104 | tf_op jit(solution)/shard_map/ppermute | solution.py:342
  16.8 0.2 turn_leading.1.near
  17.0 2.6 %collective-permute-start.7 = (bf16[2,64,256]{2,1,0:T(8,128)(2,1)S(1)}, bf16[2,64,256]{2,1,0:T(8,128)(2,1)S(1)}, u32[]{:S(2)}, u32[]{:S(2)}) collective-permute-start(bf16[2,64,256]{2,1,0:T(8,128)(2,1)S(1)} %turn_leading.1.near), channel_id=1, source_target_pairs={{0,16},{4,20},{8,24},{12,28},{16,0},{20,4},{24,8},{28,12},{1,17},{... | collective-permute-start | bytes 196616 | tf_op jit(solution)/shard_map/ppermute | solution.py:391
  19.6 4.0 %collective-permute-done.7.far = bf16[2,64,256]{2,1,0:T(8,128)(2,1)S(1)} collective-permute-done((bf16[2,64,256]{2,1,0:T(8,128)(2,1)S(1)}, bf16[2,64,256]{2,1,0:T(8,128)(2,1)S(1)}, u32[]{:S(2)}, u32[]{:S(2)}) %collective-permute-start.7) | collective-permute-done | bytes 65568 | tf_op jit(solution)/shard_map/ppermute | solution.py:391
  23.6 0.9 %collective-permute-start.12 = (bf16[2,2,64,256]{3,2,1,0:T(8,128)(2,1)S(1)}, bf16[2,2,64,256]{3,2,1,0:T(8,128)(2,1)S(1)}, u32[]{:S(2)}, u32[]{:S(2)}) collective-permute-start(bf16[2,2,64,256]{3,2,1,0:T(8,128)(2,1)S(1)} %pair.1.refs_1_.refs_0_), channel_id=1, source_target_pairs={{0,12},{4,8},{8,4},{12,0},{16,28},{20,24},{24,20},{28,16},{1,13},{... | collective-permute-start | bytes 393224 | tf_op jit(solution)/shard_map/ppermute | solution.py:402
  24.6 2.0 %collective-permute-start.11 = (bf16[2,2,64,256]{3,2,1,0:T(8,128)(2,1)S(1)}, bf16[2,2,64,256]{3,2,1,0:T(8,128)(2,1)S(1)}, u32[]{:S(2)}, u32[]{:S(2)}) collective-permute-start(bf16[2,2,64,256]{3,2,1,0:T(8,128)(2,1)S(1)} %pair.1.refs_1_.refs_0_), channel_id=1, source_target_pairs={{0,8},{4,12},{8,0},{12,4},{16,24},{20,28},{24,16},{28,20},{1,9},{5... | collective-permute-start | bytes 393224 | tf_op jit(solution)/shard_map/ppermute | solution.py:402
  26.5 0.7 %collective-permute-start.10 = (bf16[2,2,64,256]{3,2,1,0:T(8,128)(2,1)S(1)}, bf16[2,2,64,256]{3,2,1,0:T(8,128)(2,1)S(1)}, u32[]{:S(2)}, u32[]{:S(2)}) collective-permute-start(bf16[2,2,64,256]{3,2,1,0:T(8,128)(2,1)S(1)} %pair.1.refs_1_.refs_0_), channel_id=1, source_target_pairs={{0,4},{4,0},{8,12},{12,8},{16,20},{20,16},{24,28},{28,24},{1,5},{5... | collective-permute-start | bytes 393224 | tf_op jit(solution)/shard_map/ppermute | solution.py:402
  27.2 2.2 %newton.5.refs_2_ = bf16[5,256,256]{2,1,0:T(8,128)(2,1)S(1)} custom-call(f32[16,256,256]{2,1,0:T(8,128)S(1)} %get-tuple-element.44.acc, bf16[7,256,256]{2,1,0:T(8,128)(2,1)S(1)} %collective-permute-done.3.recv, bf16[5,256,256]{2,1,0:T(8,128)(2,1)S(1)} %collective-permute-done.4.refs_0_, bf16[2,2,64,256]{3,2,1,0:T(8,128)(2,1)S(1)} %pair.1.refs_1_.refs_0_), custom_call_target="tpu_custom_call" | custom-call | bytes 1048576 | tf_op jit(solution)/shard_map/newton/pallas_call | solution.py:33
  29.5 0.1 gather_rotations.1.refs_4_._
  29.7 0.3 collective-permute-done.12.refs_3_
  30.0 2.6 %collective-permute-done.11.refs_2_ = bf16[2,2,64,256]{3,2,1,0:T(8,128)(2,1)S(1)} collective-permute-done((bf16[2,2,64,256]{3,2,1,0:T(8,128)(2,1)S(1)}, bf16[2,2,64,256]{3,2,1,0:T(8,128)(2,1)S(1)}, u32[]{:S(2)}, u32[]{:S(2)}) %collective-permute-start.11) | collective-permute-done | bytes 131104 | tf_op jit(solution)/shard_map/ppermute | solution.py:402
  32.6 2.2 %turn.1 = (bf16[32,64,256]{2,1,0:T(8,128)(2,1)}, bf16[16,256,256]{2,1,0:T(8,128)(2,1)S(1)}) custom-call(s32[35]{0:T(128)S(1)} %get-tuple-element.42.refs_2_.plan_hbm, bf16[32,64,256]{2,1,0:T(8,128)(2,1)S(1)} %get-tuple-element.43.residual, bf16[5,256,256]{2,1,0:T(8,128)(2,1)S(1)} %collective-permute-done.8.main, ...), custom_call_target="tpu_custom_call", output_to_operand_aliasing={{1}: (3, {})} | custom-call | bytes 1048576 | tf_op jit(solution)/shard_map/turn/pallas_call | solution.py:33
  (16 shorter events, 0.1 us)
Async XLA Ops:
  3.4 1.5 %collective-permute-start.2 = (bf16[1,256,256]{2,1,0:T(8,128)(2,1)S(1)}, bf16[1,256,256]{2,1,0:T(8,128)(2,1)S(1)}, u32[]{:S(2)}, u32[]{:S(2)}) collective-permute-start(bf16[1,256,256]{2,1,0:T(8,128)(2,1)S(1)} %get-tuple-element.45), channel_id=1, source_target_pairs={{0,1},{1,0},{2,3},{3,2},{4,5},{5,4},{6,7},{7,6},{8,9},{9,8},{10,11... | collective-permute-start | bytes 393224 | tf_op jit(solution)/shard_map/ppermute | solution.py:342
  5.0 3.1 %collective-permute-start.3 = (bf16[7,256,256]{2,1,0:T(8,128)(2,1)S(1)}, bf16[7,256,256]{2,1,0:T(8,128)(2,1)S(1)}, u32[]{:S(2)}, u32[]{:S(2)}) collective-permute-start(bf16[7,256,256]{2,1,0:T(8,128)(2,1)S(1)} %get-tuple-element.46), channel_id=1, source_target_pairs={{0,1},{1,0},{2,3},{3,2},{4,5},{5,4},{6,7},{7,6},{8,9},{9,8},{10,11... | collective-permute-start | bytes 2752520 | tf_op jit(solution)/shard_map/ppermute | solution.py:342
  5.5 8.3 %collective-permute-start.5 = (bf16[1,256,256]{2,1,0:T(8,128)(2,1)S(1)}, bf16[1,256,256]{2,1,0:T(8,128)(2,1)S(1)}, u32[]{:S(2)}, u32[]{:S(2)}) collective-permute-start(bf16[1,256,256]{2,1,0:T(8,128)(2,1)S(1)} %get-tuple-element.48), channel_id=1, source_target_pairs={{0,2},{1,3},{2,0},{3,1},{4,6},{5,7},{6,4},{7,5},{8,10},{9,11},{10,... | collective-permute-start | bytes 393224 | tf_op jit(solution)/shard_map/ppermute | solution.py:339
  8.2 19.0 %collective-permute-start.4 = (bf16[5,256,256]{2,1,0:T(8,128)(2,1)S(1)}, bf16[5,256,256]{2,1,0:T(8,128)(2,1)S(1)}, u32[]{:S(2)}, u32[]{:S(2)}) collective-permute-start(bf16[5,256,256]{2,1,0:T(8,128)(2,1)S(1)} %chip_sums.1.refs_0_), channel_id=1, source_target_pairs={{0,2},{1,3},{2,0},{3,1},{4,6},{5,7},{6,4},{7,5},{8,10},{9,11},{10,... | collective-permute-start | bytes 1966088 | tf_op jit(solution)/shard_map/ppermute | solution.py:339
  15.4 1.4 %collective-permute-start.6 = (bf16[1,256,256]{2,1,0:T(8,128)(2,1)S(1)}, bf16[1,256,256]{2,1,0:T(8,128)(2,1)S(1)}, u32[]{:S(2)}, u32[]{:S(2)}) collective-permute-start(bf16[1,256,256]{2,1,0:T(8,128)(2,1)S(1)} %newton.4.own.refs_0_), channel_id=1, source_target_pairs={{0,1},{1,0},{2,3},{3,2},{4,5},{5,4},{6,7},{7,6},{8,9},{9,8},{10,11... | collective-permute-start | bytes 393224 | tf_op jit(solution)/shard_map/ppermute | solution.py:342
  15.5 14.0 %collective-permute-start.9 = (bf16[2,256,256]{2,1,0:T(8,128)(2,1)S(1)}, bf16[2,256,256]{2,1,0:T(8,128)(2,1)S(1)}, u32[]{:S(2)}, u32[]{:S(2)}) collective-permute-start(bf16[2,256,256]{2,1,0:T(8,128)(2,1)S(1)} %get-tuple-element.49.refs_1_), channel_id=1, source_target_pairs={{0,1},{1,0},{2,3},{3,2},{4,5},{5,4},{6,7},{7,6},{8,9},{9,8},{10,11... | collective-permute-start | bytes 786440 | tf_op jit(solution)/shard_map/ppermute | solution.py:342
  17.0 6.6 %collective-permute-start.7 = (bf16[2,64,256]{2,1,0:T(8,128)(2,1)S(1)}, bf16[2,64,256]{2,1,0:T(8,128)(2,1)S(1)}, u32[]{:S(2)}, u32[]{:S(2)}) collective-permute-start(bf16[2,64,256]{2,1,0:T(8,128)(2,1)S(1)} %turn_leading.1.near), channel_id=1, source_target_pairs={{0,16},{4,20},{8,24},{12,28},{16,0},{20,4},{24,8},{28,12},{1,17},{... | collective-permute-start | bytes 196616 | tf_op jit(solution)/shard_map/ppermute | solution.py:391
  23.6 6.3 %collective-permute-start.12 = (bf16[2,2,64,256]{3,2,1,0:T(8,128)(2,1)S(1)}, bf16[2,2,64,256]{3,2,1,0:T(8,128)(2,1)S(1)}, u32[]{:S(2)}, u32[]{:S(2)}) collective-permute-start(bf16[2,2,64,256]{3,2,1,0:T(8,128)(2,1)S(1)} %pair.1.refs_1_.refs_0_), channel_id=1, source_target_pairs={{0,12},{4,8},{8,4},{12,0},{16,28},{20,24},{24,20},{28,16},{1,13},{... | collective-permute-start | bytes 393224 | tf_op jit(solution)/shard_map/ppermute | solution.py:402
  24.6 8.0 %collective-permute-start.11 = (bf16[2,2,64,256]{3,2,1,0:T(8,128)(2,1)S(1)}, bf16[2,2,64,256]{3,2,1,0:T(8,128)(2,1)S(1)}, u32[]{:S(2)}, u32[]{:S(2)}) collective-permute-start(bf16[2,2,64,256]{3,2,1,0:T(8,128)(2,1)S(1)} %pair.1.refs_1_.refs_0_), channel_id=1, source_target_pairs={{0,8},{4,12},{8,0},{12,4},{16,24},{20,28},{24,16},{28,20},{1,9},{5... | collective-permute-start | bytes 393224 | tf_op jit(solution)/shard_map/ppermute | solution.py:402
  26.5 6.1 %collective-permute-start.10 = (bf16[2,2,64,256]{3,2,1,0:T(8,128)(2,1)S(1)}, bf16[2,2,64,256]{3,2,1,0:T(8,128)(2,1)S(1)}, u32[]{:S(2)}, u32[]{:S(2)}) collective-permute-start(bf16[2,2,64,256]{3,2,1,0:T(8,128)(2,1)S(1)} %pair.1.refs_1_.refs_0_), channel_id=1, source_target_pairs={{0,4},{4,0},{8,12},{12,8},{16,20},{20,16},{24,28},{28,24},{1,5},{5... | collective-permute-start | bytes 393224 | tf_op jit(solution)/shard_map/ppermute | solution.py:402
  29.4 3.2 %collective-permute-start.8 = (bf16[5,256,256]{2,1,0:T(8,128)(2,1)S(1)}, bf16[5,256,256]{2,1,0:T(8,128)(2,1)S(1)}, u32[]{:S(2)}, u32[]{:S(2)}) collective-permute-start(bf16[5,256,256]{2,1,0:T(8,128)(2,1)S(1)} %newton.5.refs_2_), channel_id=1, source_target_pairs={{0,1},{1,0},{2,3},{3,2},{4,5},{5,4},{6,7},{7,6},{8,9},{9,8},{10,11... | collective-permute-start | bytes 1966088 | tf_op jit(solution)/shard_map/ppermute | solution.py:342
  32.6 2.2 %copy-start = (f32[16,256]{1,0:T(8,128)S(1)}, f32[16,256]{1,0:T(8,128)}, u32[]{:S(2)}) copy-start(f32[16,256]{1,0:T(8,128)} %centroids_hbm.1) | copy-start | bytes 49156
  32.6 2.2 %copy-start.1 = (s32[32]{0:T(128)S(1)}, s32[32]{0:T(128)}, u32[]{:S(2)}) copy-start(s32[32]{0:T(128)} %bl_hbm.1) | copy-start | bytes 388
  32.6 2.2 %copy-start.2 = (s32[32]{0:T(128)S(1)}, s32[32]{0:T(128)}, u32[]{:S(2)}) copy-start(s32[32]{0:T(128)} %ln_hbm.1) | copy-start | bytes 388
